TPU v7x, 32 devices: a whole 2x2x4 slice. The times are simulated.
32 devices in a mesh: rows: 16 (over z, y, core), chan: 2 (over x).
Axes of the slice: x: 2, y: 2, z: 4, core: 2. Of those that a mesh axis runs over, the one named last changes fastest.
Arguments:
- features: bfloat16 [64, 128, 2048], P('rows', None, 'chan'), may hold values from 0 to 12, as said below
- low_features: bfloat16 [256, 512, 256], P('rows', 'chan'), may hold values from -6 to 6
- w_one: bfloat16 [2048, 256], P('chan'), may hold values from -0.125 to 0.125
- w_rate: bfloat16 [3, 9, 2048, 256], P(None, None, 'chan', 'rows'), may hold values from -0.046875 to 0.046875
- w_pool: bfloat16 [2048, 256], P('chan'), may hold values from -0.125 to 0.125
- b_branch: float32 [5, 256], replicated, may hold values from -3 to 3
- w_proj: bfloat16 [1280, 256], replicated, may hold values from -0.15625 to 0.15625
- b_proj: float32 [256], replicated, may hold values from -3 to 3
- w_low: bfloat16 [256, 48], replicated, may hold values from -0.375 to 0.375
- b_low: float32 [48], replicated, may hold values from -3 to 3
- w_dec_up: bfloat16 [9, 256, 256], replicated, may hold values from -0.109375 to 0.109375
- w_dec_low: bfloat16 [9, 48, 256], replicated, may hold values from -0.109375 to 0.109375
- b_dec: float32 [256], replicated, may hold values from -3 to 3
Outputs:
- context: bfloat16 [64, 128, 256], P('rows', 'chan')
- decoded: bfloat16 [256, 512, 256], P('rows', 'chan')
Inputs may be any that keep to these rules, and one draw needn't show every extreme that they name: features are nonnegative.
All inputs are finite; a program needn't handle non-finite values.
Results may differ from a plain program's by a relative error of at most 0.019.
Values may be sent and summed in bfloat16 or wider, within the bound.
A program may use at most 128 MiB of HBM per device.

v0:
```python
import jax
import jax.numpy as jnp
from jax import lax
from jax.sharding import PartitionSpec as P

RATE = 6


BLEND = (0.875, 0.625, 0.375, 0.125)


def passed_along(block, axis, distance):
    devices = range(lax.axis_size(axis))
    route = [(i - distance, i) for i in devices if i - distance in devices]
    return lax.ppermute(block, axis, route)


def padded_2(array, sides, width):
    for axis, dim in sides:
        devices, length = (lax.axis_size(axis), array.shape[dim])
        up = [(i, (i + 1) % devices) for i in range(devices - 1)]
        down = [(j, i) for i, j in up]
        last = lax.slice_in_dim(array, length - width, length, axis=dim)
        first = lax.slice_in_dim(array, 0, width, axis=dim)
        before = lax.ppermute(last, axis, up)
        after = lax.ppermute(first, axis, down)
        array = jnp.concatenate([before, array, after], axis=dim)
    return array


def move_cols(field, across):
    extent = field.shape[1]
    amount = abs(across)
    padded = jnp.pad(field, ((0, 0), (amount, amount), (0, 0)))
    return padded[:, amount + across : amount + across + extent]


def fetch_rows(features, offset):
    hop_count, remain = divmod(offset, features.shape[0])
    upper_part = features[remain:]
    upper_part = passed_along(upper_part, "rows", -hop_count)
    if remain == 0:
        return upper_part
    lower_part = features[:remain]
    lower_part = passed_along(lower_part, "rows", -hop_count - 1)
    return jnp.concatenate([upper_part, lower_part], axis=0)


def rate_matrix(features, spacing):
    sources = (fetch_rows(features, -spacing), features, fetch_rows(features, spacing))
    pieces = [
        move_cols(source, (col_step - 1) * spacing) for source in sources for col_step in range(3)
    ]
    stacked = jnp.concatenate(pieces, axis=2)
    return stacked.reshape(-1, stacked.shape[2])


def blend_axis(field, axis_pos):
    count_in = field.shape[axis_pos]
    lower_half = lax.slice_in_dim(field, 0, count_in - 1, axis=axis_pos)
    upper_half = lax.slice_in_dim(field, 1, count_in, axis=axis_pos)
    blended = jnp.stack(
        [factor * lower_half + (1.0 - factor) * upper_half for factor in BLEND], axis=axis_pos + 1
    )
    target = list(lower_half.shape)
    target[axis_pos] = 4 * (count_in - 1)
    return blended.reshape(target)


def edge_copy(padded, rows_index, rows_count, chan_index, chan_count):
    top_row = jnp.where(rows_index == 0, padded[1:2], padded[0:1])
    bottom_row = jnp.where(rows_index == rows_count - 1, padded[-2:-1], padded[-1:])
    padded = jnp.concatenate([top_row, padded[1:-1], bottom_row], axis=0)
    left_col = jnp.where(chan_index == 0, padded[:, 1:2], padded[:, 0:1])
    right_col = jnp.where(chan_index == chan_count - 1, padded[:, -2:-1], padded[:, -1:])
    return jnp.concatenate([left_col, padded[:, 1:-1], right_col], axis=1)


def tap_matrix(padded, out_rows, out_cols):
    pieces = [
        padded[row_step : row_step + out_rows, col_step : col_step + out_cols]
        for row_step in range(3)
        for col_step in range(3)
    ]
    stacked = jnp.concatenate(pieces, axis=2)
    return stacked.reshape(out_rows * out_cols, -1)


def on_device(
    features,
    low_features,
    w_one,
    w_rate,
    w_pool,
    b_branch,
    w_proj,
    b_proj,
    w_low,
    b_low,
    w_dec_up,
    w_dec_low,
    b_dec,
):
    strip_rows, map_cols, group_in = features.shape
    branch_width = w_one.shape[1]
    pixel_count = strip_rows * map_cols
    rows_index = lax.axis_index("rows")
    rows_count = lax.axis_size("rows")
    chan_index = lax.axis_index("chan")
    chan_count = lax.axis_size("chan")
    local_sum = jnp.sum(features, axis=(0, 1), dtype=jnp.float32)
    map_total = strip_rows * rows_count * map_cols
    pool_weight = w_pool.astype(jnp.float32)
    pooled = lax.psum(local_sum, "rows") / map_total
    local_term = jnp.dot(pooled, pool_weight, precision=lax.Precision.HIGHEST)
    pool_pre = lax.psum(local_term, "chan")
    pool_branch = jax.nn.relu(pool_pre + b_branch[4]).astype(jnp.bfloat16)
    head_weight = w_proj[: 4 * branch_width]
    pool_term = jnp.dot(
        pool_branch[None, :], w_proj[4 * branch_width :], preferred_element_type=jnp.float32
    )[0]
    rate_all = lax.all_gather(w_rate, "rows", axis=3, tiled=True)
    rate_outputs = []
    for rate_level in range(3):
        matrix = rate_matrix(features, RATE * (rate_level + 1))
        weight_flat = rate_all[rate_level].reshape(-1, rate_all.shape[3])
        rate_outputs.append(jnp.dot(matrix, weight_flat, preferred_element_type=jnp.float32))
    one_out = jnp.dot(
        features.reshape(pixel_count, group_in), w_one, preferred_element_type=jnp.float32
    )
    partial_value = jnp.concatenate([one_out] + rate_outputs, axis=1).reshape(
        strip_rows, map_cols, 4 * branch_width
    )
    conv_bias = b_branch[:4].reshape(-1)
    summed = lax.psum_scatter(
        partial_value.astype(jnp.bfloat16), "chan", scatter_dimension=2, tiled=True
    ).astype(jnp.float32)
    share_width = summed.shape[2]
    bias_share = lax.dynamic_slice_in_dim(conv_bias, chan_index * share_width, share_width)
    branches = jax.nn.relu(summed + bias_share).astype(jnp.bfloat16)
    weight_share = lax.dynamic_slice_in_dim(head_weight, chan_index * share_width, share_width, 0)
    partial_terms = jnp.dot(
        branches.reshape(-1, share_width), weight_share, preferred_element_type=jnp.float32
    )
    partial_terms = partial_terms.reshape(strip_rows, map_cols, branch_width)
    projected = lax.psum_scatter(
        partial_terms.astype(jnp.bfloat16), "chan", scatter_dimension=1, tiled=True
    ).astype(jnp.float32)
    context = jax.nn.relu(projected + pool_term + b_proj).astype(jnp.bfloat16)
    tile_rows_count = context.shape[0]
    tile_cols_count = context.shape[1]
    fine_rows, fine_cols = (low_features.shape[0], low_features.shape[1])
    low_flat = low_features.reshape(fine_rows * fine_cols, low_features.shape[2])
    low_mapped = jax.nn.relu(
        jnp.dot(low_flat, w_low, preferred_element_type=jnp.float32) + b_low
    ).astype(jnp.bfloat16)
    low_mapped = low_mapped.reshape(fine_rows, fine_cols, -1)
    coarse = padded_2(context, (("rows", 0), ("chan", 1)), 1)
    coarse = edge_copy(coarse, rows_index, rows_count, chan_index, chan_count).astype(jnp.float32)
    upsampled = blend_axis(coarse, 0)[1 : 4 * tile_rows_count + 3]
    upsampled = blend_axis(upsampled, 1)[:, 1 : 4 * tile_cols_count + 3]
    ext_rows, ext_cols = (upsampled.shape[0], upsampled.shape[1])
    row_pos = lax.broadcasted_iota(jnp.int32, (ext_rows, 1, 1), 0)
    col_pos = lax.broadcasted_iota(jnp.int32, (1, ext_cols, 1), 1)
    inside = ((row_pos > 0) | (rows_index > 0)) & (
        (row_pos < ext_rows - 1) | (rows_index < rows_count - 1)
    )
    inside = (
        inside
        & ((col_pos > 0) | (chan_index > 0))
        & ((col_pos < ext_cols - 1) | (chan_index < chan_count - 1))
    )
    up_pad = jnp.where(inside, upsampled, 0.0).astype(jnp.bfloat16)
    low_pad = padded_2(low_mapped, (("rows", 0), ("chan", 1)), 1)
    up_taps = tap_matrix(up_pad, fine_rows, fine_cols)
    low_taps = tap_matrix(low_pad, fine_rows, fine_cols)
    mixed = jnp.dot(
        up_taps, w_dec_up.reshape(-1, w_dec_up.shape[2]), preferred_element_type=jnp.float32
    )
    mixed = mixed + jnp.dot(
        low_taps, w_dec_low.reshape(-1, w_dec_low.shape[2]), preferred_element_type=jnp.float32
    )
    decoded = jax.nn.relu(mixed + b_dec).astype(jnp.bfloat16).reshape(fine_rows, fine_cols, -1)
    return (context, decoded)


def solution(mesh):
    in_specs = (
        P("rows", None, "chan"),
        P("rows", "chan", None),
        P("chan", None),
        P(None, None, "chan", "rows"),
        P("chan", None),
        P(),
        P(),
        P(),
        P(),
        P(),
        P(),
        P(),
        P(),
    )
    out_specs = (P("rows", "chan", None), P("rows", "chan", None))
    return jax.shard_map(
        on_device, mesh=mesh, in_specs=in_specs, out_specs=out_specs, check_vma=False
    )
```

profile of v0, /device:TPU:1, one launch (start us, length us, event | category | flops | bytes accessed | tf_op | source)
XLA Modules:
  0.0 369.0 jit_solution(13173273247153160039)
XLA Ops:
  8.0 5.7 %collective-permute-start.4 = (bf16[4,128,1024]{2,1,0:T(8,128)(2,1)}, bf16[4,128,1024]{2,1,0:T(8,128)(2,1)}, u32[]{:S(2)}, u32[]{:S(2)}) collective-permute-start(bf16[4,128,1024]{2,1,0:T(8,128)(2,1)} %param.13), channel_id=1, source_target_pairs={{0,6},{2,8},{4,10},{6,12},{8,14},{10,16},{12,18},{14,20},{16,22},{... | collective-permute-start | bytes 3145736 | tf_op jit(solution)/shard_map/ppermute | solution.py:15
  15.9 2.8 collective-permute-start.1
  18.8 3.0 collective-permute-start
  25.3 3.5 collective-permute-start.14
  29.0 72.2 %psum.14 = f32[1024]{0:T(1024)S(1)} all-reduce(f32[1024]{0:T(1024)S(1)} %convert_reduce_fusion), channel_id=1, replica_groups=mesh['rows'=16,'chan'=2] {'rows'}, use_global_device_ids=true, to_apply=%region_3.4 | all-reduce | flops 1024 | bytes 8192 | tf_op jit(solution)/shard_map/psum | solution.py:114
  102.5 4.2 %psum.15 = f32[256]{0:T(256)S(1)} all-reduce(f32[256]{0:T(256)S(1)} %bitcast.132), channel_id=1, replica_groups=mesh['rows'=16,'chan'=2] {'chan'}, use_global_device_ids=true, to_apply=%region_4.5 | all-reduce | flops 256 | bytes 2048 | tf_op jit(solution)/shard_map/psum | solution.py:116
  114.6 4.0 %collective-permute-start.16 = (bf16[18,1,48]{1,0,2:T(8,128)(2,1)S(1)}, bf16[18,1,48]{1,0,2:T(8,128)(2,1)S(1)}, u32[]{:S(2)}, u32[]{:S(2)}) collective-permute-start(bf16[18,1,48]{1,0,2:T(8,128)(2,1)S(1)} %get-tuple-element.26), channel_id=1, source_target_pairs={{0,1},{2,3},{4,5},{6,7},{8,9},{10,11},{12,13},{14,15},{16,17},{18,... | collective-permute-start | bytes 5192 | tf_op jit(solution)/shard_map/ppermute | solution.py:25
  122.9 4.6 %collective-permute-start.7 = (bf16[2,128,1024]{2,1,0:T(8,128)(2,1)}, bf16[2,128,1024]{2,1,0:T(8,128)(2,1)S(1)}, u32[]{:S(2)}, u32[]{:S(2)}) collective-permute-start(bf16[2,128,1024]{2,1,0:T(8,128)(2,1)} %get-tuple-element.18), channel_id=1, source_target_pairs={{0,8},{2,10},{4,12},{6,14},{8,16},{10,18},{12,20},{14,22},{16,24},... | collective-permute-start | bytes 1572872 | tf_op jit(solution)/shard_map/ppermute | solution.py:15
  127.5 6.1 %collective-permute-start.6 = (bf16[2,128,1024]{2,1,0:T(8,128)(2,1)}, bf16[2,128,1024]{2,1,0:T(8,128)(2,1)S(1)}, u32[]{:S(2)}, u32[]{:S(2)}) collective-permute-start(bf16[2,128,1024]{2,1,0:T(8,128)(2,1)} %get-tuple-element.17), channel_id=1, source_target_pairs={{0,10},{2,12},{4,14},{6,16},{8,18},{10,20},{12,22},{14,24},{16,26}... | collective-permute-start | bytes 1572872 | tf_op jit(solution)/shard_map/ppermute | solution.py:15
  144.4 5.6 %collective-permute-done.7 = bf16[2,128,1024]{2,1,0:T(8,128)(2,1)S(1)} collective-permute-done((bf16[2,128,1024]{2,1,0:T(8,128)(2,1)}, bf16[2,128,1024]{2,1,0:T(8,128)(2,1)S(1)}, u32[]{:S(2)}, u32[]{:S(2)}) %collective-permute-start.7) | collective-permute-done | bytes 524320 | tf_op jit(solution)/shard_map/ppermute | solution.py:15
  151.3 13.7 %collective-permute-done.6 = bf16[2,128,1024]{2,1,0:T(8,128)(2,1)S(1)} collective-permute-done((bf16[2,128,1024]{2,1,0:T(8,128)(2,1)}, bf16[2,128,1024]{2,1,0:T(8,128)(2,1)S(1)}, u32[]{:S(2)}, u32[]{:S(2)}) %collective-permute-start.6) | collective-permute-done | bytes 524320 | tf_op jit(solution)/shard_map/ppermute | solution.py:15
  165.0 3.0 collective-permute-start.2
  189.8 15.8 %collective-permute-done.5 = bf16[4,128,1024]{2,1,0:T(8,128)(2,1)S(1)} collective-permute-done((bf16[4,128,1024]{2,1,0:T(8,128)(2,1)S(1)}, bf16[4,128,1024]{2,1,0:T(8,128)(2,1)S(1)}, u32[]{:S(2)}, u32[]{:S(2)}) %collective-permute-start.5) | collective-permute-done | bytes 1048608 | tf_op jit(solution)/shard_map/ppermute | solution.py:15
  206.6 3.3 copy-done.14
  209.8 3.6 copy-done.13
  214.7 10.8 %fusion.34 = (bf16[1,9,1024,256]{2,3,1,0:T(8,128)(2,1)}, bf16[1,9,1024,256]{2,3,1,0:T(8,128)(2,1)}, bf16[1,9,1024,256]{2,3,1,0:T(8,128)(2,1)}) fusion(bf16[3,9,1024,256]{2,3,1,0:T(8,128)(2,1)} %all-gather.2.cloned.1.call-done), kind=kLoop, calls=%fused_computation.135 | loop fusion | bytes 28311552 | tf_op jit(solution)/shard_map/slice | solution.py:126
  225.5 6.7 %copy.51 = bf16[1,9,1024,256]{3,2,1,0:T(8,128)(2,1)} copy(bf16[1,9,1024,256]{2,3,1,0:T(8,128)(2,1)} %get-tuple-element.4) | data formatting | bytes 9437184
  232.1 6.7 %copy.50 = bf16[1,9,1024,256]{3,2,1,0:T(8,128)(2,1)} copy(bf16[1,9,1024,256]{2,3,1,0:T(8,128)(2,1)} %get-tuple-element.3) | data formatting | bytes 9437184
  238.8 6.7 %copy.49 = bf16[1,9,1024,256]{3,2,1,0:T(8,128)(2,1)} copy(bf16[1,9,1024,256]{2,3,1,0:T(8,128)(2,1)} %get-tuple-element.2) | data formatting | bytes 9437184
  245.5 7.8 %convolution_convert_fusion = bf16[512,256]{0,1:T(8,128)(2,1)S(1)} fusion(bf16[512,9216]{1,0:T(8,128)(2,1)} %bitcast.127, bf16[9216,256]{1,0:T(8,128)(2,1)} %bitcast.107), kind=kOutput, calls=%fused_computation.37 | convolution fusion | flops 2416050176 | bytes 14417920 | tf_op jit(solution)/shard_map/dot_general | solution.py:127
  253.4 6.4 %convolution_convert_fusion.1 = bf16[512,256]{0,1:T(8,128)(2,1)S(1)} fusion(bf16[512,9216]{1,0:T(8,128)(2,1)} %bitcast.128, bf16[9216,256]{1,0:T(8,128)(2,1)S(1)} %bitcast.103), kind=kOutput, calls=%fused_computation.38 | convolution fusion | flops 2416050176 | bytes 14417920 | tf_op jit(solution)/shard_map/dot_general | solution.py:127
  259.8 6.4 %convolution_convert_fusion.2 = bf16[512,256]{0,1:T(8,128)(2,1)S(1)} fusion(bf16[512,9216]{1,0:T(8,128)(2,1)} %bitcast.1, bf16[9216,256]{1,0:T(8,128)(2,1)S(1)} %bitcast.106), kind=kOutput, calls=%fused_computation.39 | convolution fusion | flops 2416050176 | bytes 14417920 | tf_op jit(solution)/shard_map/dot_general | solution.py:127
  272.7 21.3 %reduce-scatter.3.cloned.1.call-done = bf16[4,128,512]{2,1,0:T(8,128)(2,1)} async-done(((bf16[4,128,1024]{2,1,0:T(8,128)(2,1)}), bf16[4,128,512]{2,1,0:T(8,128)(2,1)}) %reduce-scatter.3.cloned.1.call-update) | async-done | bytes 524304 | tf_op jit(solution)/shard_map/reduce_scatter | solution.py:135
  297.8 10.7 %reduce-scatter.5.cloned.1.call-done = bf16[4,64,256]{2,1,0:T(8,128)(2,1)} async-done(((bf16[4,128,256]{2,1,0:T(8,128)(2,1)}), bf16[4,64,256]{2,1,0:T(8,128)(2,1)}) %reduce-scatter.5.cloned.1.call-update) | async-done | bytes 131088 | tf_op jit(solution)/shard_map/reduce_scatter | solution.py:146
  309.6 2.6 collective-permute-start.11
  312.2 3.0 collective-permute-start.10
  317.5 15.3 %collective-permute-start.12 = (bf16[6,1,256]{2,1,0:T(2,128)(2,1)S(1)}, bf16[6,1,256]{2,1,0:T(2,128)(2,1)S(1)}, u32[]{:S(2)}, u32[]{:S(2)}) collective-permute-start(bf16[6,1,256]{2,1,0:T(2,128)(2,1)S(1)} %get-tuple-element.39), channel_id=1, source_target_pairs={{0,1},{2,3},{4,5},{6,7},{8,9},{10,11},{12,13},{14,15},{16,17},{18,... | collective-permute-start | bytes 9224 | tf_op jit(solution)/shard_map/ppermute | solution.py:25
  335.4 2.7 copy.43
  338.1 5.1 %reshape.154 = bf16[18,260,256]{2,1,0:T(8,128)(2,1)} reshape(bf16[18,65,4,256]{3,2,1,0:T(4,128)(2,1)} %copy.43) | data formatting | bytes 4792320 | tf_op jit(solution)/shard_map/reshape | solution.py:67
  343.2 3.1 fusion.3
  351.7 5.6 %fusion.41 = f32[4096,256]{1,0:T(8,128)S(1)} fusion(bf16[4096,2304]{1,0:T(8,128)(2,1)S(1)} %bitcast.126, bf16[2304,256]{1,0:T(8,128)(2,1)S(1)} %bitcast.134), kind=kOutput, calls=%fused_computation.142 | convolution fusion | flops 4831838208 | bytes 24248320 | tf_op jit(solution)/shard_map/dot_general | solution.py:177
  357.4 4.9 %fusion.2 = bf16[4096,256]{1,0:T(8,128)(2,1)} fusion(f32[4096,256]{1,0:T(8,128)S(1)} %fusion.41, bf16[4096,432]{0,1:T(8,128)(2,1)} %constant_dynamic-update-slice_fusion.13, bf16[432,256]{1,0:T(8,128)(2,1)S(1)} %bitcast.135, f32[256]{0:T(256)S(1)} %copy-done.20), kind=kOutput, calls=%fused_computation.4 | convolution fusion | flops 910163968 | bytes 10052608 | tf_op jit(solution)/shard_map/dot_general | solution.py:180
  (174 shorter events, 77.4 us)
Async XLA Ops:
  7.2 14.5 %copy-start = (bf16[16,256,256]{2,1,0:T(8,128)(2,1)S(1)}, bf16[16,256,256]{2,1,0:T(8,128)(2,1)}, u32[]{:S(2)}) copy-start(bf16[16,256,256]{2,1,0:T(8,128)(2,1)} %param.14) | copy-start | bytes 6291460
  7.2 21.6 %copy-start.2 = (bf16[4,128,1024]{2,1,0:T(8,128)(2,1)S(1)}, bf16[4,128,1024]{2,1,0:T(8,128)(2,1)}, u32[]{:S(2)}) copy-start(bf16[4,128,1024]{2,1,0:T(8,128)(2,1)} %param.13) | copy-start | bytes 3145732
  7.2 21.6 %copy-start.15 = (f32[5,256]{1,0:T(8,128)S(1)}, f32[5,256]{1,0:T(8,128)}, u32[]{:S(2)}) copy-start(f32[5,256]{1,0:T(8,128)} %param.18) | copy-start | bytes 15364
  7.2 207.5 %all-gather.2.cloned.1.call-start = ((), (), s32[]{:S(2)}) async-start(), calls=%async_computation.2 | async-start | bytes 15040512 | tf_op jit(solution)/shard_map/all_gather | solution.py:122
  7.9 286.1 %reduce-scatter.3.cloned.1.call-start = ((), (), s32[]{:S(2)}) async-start(), calls=%async_computation.3 | async-start | bytes 1572864 | tf_op jit(solution)/shard_map/reduce_scatter | solution.py:135
  8.0 170.0 %collective-permute-start.4 = (bf16[4,128,1024]{2,1,0:T(8,128)(2,1)}, bf16[4,128,1024]{2,1,0:T(8,128)(2,1)}, u32[]{:S(2)}, u32[]{:S(2)}) collective-permute-start(bf16[4,128,1024]{2,1,0:T(8,128)(2,1)} %param.13), channel_id=1, source_target_pairs={{0,6},{2,8},{4,10},{6,12},{8,14},{10,16},{12,18},{14,20},{16,22},{... | collective-permute-start | bytes 3145736 | tf_op jit(solution)/shard_map/ppermute | solution.py:15
  15.9 124.3 %collective-permute-start.1 = (bf16[2,128,1024]{2,1,0:T(8,128)(2,1)}, bf16[2,128,1024]{2,1,0:T(8,128)(2,1)}, u32[]{:S(2)}, u32[]{:S(2)}) collective-permute-start(bf16[2,128,1024]{2,1,0:T(8,128)(2,1)} %get-tuple-element.18), channel_id=1, source_target_pairs={{0,2},{2,4},{4,6},{6,8},{8,10},{10,12},{12,14},{14,16},{16,18},{18... | collective-permute-start | bytes 1572872 | tf_op jit(solution)/shard_map/ppermute | solution.py:15
  18.8 122.8 %collective-permute-start = (bf16[2,128,1024]{2,1,0:T(8,128)(2,1)}, bf16[2,128,1024]{2,1,0:T(8,128)(2,1)}, u32[]{:S(2)}, u32[]{:S(2)}) collective-permute-start(bf16[2,128,1024]{2,1,0:T(8,128)(2,1)} %get-tuple-element.17), channel_id=1, source_target_pairs={{0,4},{2,6},{4,8},{6,10},{8,12},{10,14},{12,16},{14,18},{16,20},{1... | collective-permute-start | bytes 1572872 | tf_op jit(solution)/shard_map/ppermute | solution.py:15
  23.2 89.5 %collective-permute-start.15 = (bf16[1,256,48]{1,2,0:T(8,128)(2,1)S(1)}, bf16[1,256,48]{1,2,0:T(8,128)(2,1)S(1)}, u32[]{:S(2)}, u32[]{:S(2)}) collective-permute-start(bf16[1,256,48]{1,2,0:T(8,128)(2,1)S(1)} %get-tuple-element.36), channel_id=1, source_target_pairs={{2,0},{4,2},{6,4},{8,6},{10,8},{12,10},{14,12},{16,14},{18,16},{20... | collective-permute-start | bytes 73736 | tf_op jit(solution)/shard_map/ppermute | solution.py:26
  25.3 87.5 %collective-permute-start.14 = (bf16[1,256,48]{1,2,0:T(8,128)(2,1)S(1)}, bf16[1,256,48]{1,2,0:T(8,128)(2,1)S(1)}, u32[]{:S(2)}, u32[]{:S(2)}) collective-permute-start(bf16[1,256,48]{1,2,0:T(8,128)(2,1)S(1)} %get-tuple-element.35), channel_id=1, source_target_pairs={{0,2},{2,4},{4,6},{6,8},{8,10},{10,12},{12,14},{14,16},{16,18},{18... | collective-permute-start | bytes 73736 | tf_op jit(solution)/shard_map/ppermute | solution.py:25
  113.3 9.6 %collective-permute-start.17 = (bf16[18,1,48]{1,0,2:T(8,128)(2,1)S(1)}, bf16[18,1,48]{1,0,2:T(8,128)(2,1)S(1)}, u32[]{:S(2)}, u32[]{:S(2)}) collective-permute-start(bf16[18,1,48]{1,0,2:T(8,128)(2,1)S(1)} %get-tuple-element.25), channel_id=1, source_target_pairs={{1,0},{3,2},{5,4},{7,6},{9,8},{11,10},{13,12},{15,14},{17,16},{19,... | collective-permute-start | bytes 5192 | tf_op jit(solution)/shard_map/ppermute | solution.py:26
  114.6 12.9 %collective-permute-start.16 = (bf16[18,1,48]{1,0,2:T(8,128)(2,1)S(1)}, bf16[18,1,48]{1,0,2:T(8,128)(2,1)S(1)}, u32[]{:S(2)}, u32[]{:S(2)}) collective-permute-start(bf16[18,1,48]{1,0,2:T(8,128)(2,1)S(1)} %get-tuple-element.26), channel_id=1, source_target_pairs={{0,1},{2,3},{4,5},{6,7},{8,9},{10,11},{12,13},{14,15},{16,17},{18,... | collective-permute-start | bytes 5192 | tf_op jit(solution)/shard_map/ppermute | solution.py:25
  122.9 27.0 %collective-permute-start.7 = (bf16[2,128,1024]{2,1,0:T(8,128)(2,1)}, bf16[2,128,1024]{2,1,0:T(8,128)(2,1)S(1)}, u32[]{:S(2)}, u32[]{:S(2)}) collective-permute-start(bf16[2,128,1024]{2,1,0:T(8,128)(2,1)} %get-tuple-element.18), channel_id=1, source_target_pairs={{0,8},{2,10},{4,12},{6,14},{8,16},{10,18},{12,20},{14,22},{16,24},... | collective-permute-start | bytes 1572872 | tf_op jit(solution)/shard_map/ppermute | solution.py:15
  127.5 37.5 %collective-permute-start.6 = (bf16[2,128,1024]{2,1,0:T(8,128)(2,1)}, bf16[2,128,1024]{2,1,0:T(8,128)(2,1)S(1)}, u32[]{:S(2)}, u32[]{:S(2)}) collective-permute-start(bf16[2,128,1024]{2,1,0:T(8,128)(2,1)} %get-tuple-element.17), channel_id=1, source_target_pairs={{0,10},{2,12},{4,14},{6,16},{8,18},{10,20},{12,22},{14,24},{16,26}... | collective-permute-start | bytes 1572872 | tf_op jit(solution)/shard_map/ppermute | solution.py:15
  140.3 35.8 %collective-permute-start.9 = (bf16[2,128,1024]{2,1,0:T(8,128)(2,1)}, bf16[2,128,1024]{2,1,0:T(8,128)(2,1)S(1)}, u32[]{:S(2)}, u32[]{:S(2)}) collective-permute-start(bf16[2,128,1024]{2,1,0:T(8,128)(2,1)} %get-tuple-element.18), channel_id=1, source_target_pairs={{10,0},{12,2},{14,4},{16,6},{18,8},{20,10},{22,12},{24,14},{26,16}... | collective-permute-start | bytes 1572872 | tf_op jit(solution)/shard_map/ppermute | solution.py:15
  141.6 34.5 %collective-permute-start.8 = (bf16[2,128,1024]{2,1,0:T(8,128)(2,1)}, bf16[2,128,1024]{2,1,0:T(8,128)(2,1)S(1)}, u32[]{:S(2)}, u32[]{:S(2)}) collective-permute-start(bf16[2,128,1024]{2,1,0:T(8,128)(2,1)} %get-tuple-element.17), channel_id=1, source_target_pairs={{8,0},{10,2},{12,4},{14,6},{16,8},{18,10},{20,12},{22,14},{24,16},... | collective-permute-start | bytes 1572872 | tf_op jit(solution)/shard_map/ppermute | solution.py:15
  150.0 23.5 %collective-permute-start.3 = (bf16[2,128,1024]{2,1,0:T(8,128)(2,1)}, bf16[2,128,1024]{2,1,0:T(8,128)(2,1)S(1)}, u32[]{:S(2)}, u32[]{:S(2)}) collective-permute-start(bf16[2,128,1024]{2,1,0:T(8,128)(2,1)} %get-tuple-element.18), channel_id=1, source_target_pairs={{4,0},{6,2},{8,4},{10,6},{12,8},{14,10},{16,12},{18,14},{20,16},{2... | collective-permute-start | bytes 1572872 | tf_op jit(solution)/shard_map/ppermute | solution.py:15
  165.0 10.7 %collective-permute-start.2 = (bf16[2,128,1024]{2,1,0:T(8,128)(2,1)}, bf16[2,128,1024]{2,1,0:T(8,128)(2,1)S(1)}, u32[]{:S(2)}, u32[]{:S(2)}) collective-permute-start(bf16[2,128,1024]{2,1,0:T(8,128)(2,1)} %get-tuple-element.17), channel_id=1, source_target_pairs={{2,0},{4,2},{6,4},{8,6},{10,8},{12,10},{14,12},{16,14},{18,16},{20... | collective-permute-start | bytes 1572872 | tf_op jit(solution)/shard_map/ppermute | solution.py:15
  173.4 32.2 %collective-permute-start.5 = (bf16[4,128,1024]{2,1,0:T(8,128)(2,1)S(1)}, bf16[4,128,1024]{2,1,0:T(8,128)(2,1)S(1)}, u32[]{:S(2)}, u32[]{:S(2)}) collective-permute-start(bf16[4,128,1024]{2,1,0:T(8,128)(2,1)S(1)} %copy-done.2), channel_id=1, source_target_pairs={{6,0},{8,2},{10,4},{12,6},{14,8},{16,10},{18,12},{20,14},{22,16},{... | collective-permute-start | bytes 3145736 | tf_op jit(solution)/shard_map/ppermute | solution.py:15
  245.5 14.2 %slice-start = ((s8[4718592]{0:T(1024)(128)(4,1)}), s8[4194304]{0:T(1024)(128)(4,1)S(1)}, s32[]{:S(2)}) async-start(s8[4718592]{0:T(1024)(128)(4,1)} %bitcast.104), calls=%async_computation.5 | async-start | bytes 8388608
  266.3 27.7 %copy-start.16 = (f32[512]{0:T(512)S(1)}, f32[512]{0:T(512)}, u32[]{:S(2)}) copy-start(f32[512]{0:T(512)} %dynamic_slice.6) | copy-start | bytes 6148
  267.6 28.5 %copy-start.9 = (bf16[6,8,16,256]{3,1,2,0:T(8,128)(2,1)S(1)}, bf16[6,8,16,256]{3,1,2,0:T(8,128)(2,1)}, u32[]{:S(2)}) copy-start(bf16[6,8,16,256]{3,1,2,0:T(8,128)(2,1)} %copy.58) | copy-start | bytes 1179652
  267.6 29.3 %copy-start.8 = (bf16[16,256,48]{1,0,2:T(8,128)(2,1)S(1)}, bf16[16,256,48]{1,0,2:T(8,128)(2,1)}, u32[]{:S(2)}) copy-start(bf16[16,256,48]{1,0,2:T(8,128)(2,1)} %get-tuple-element.49) | copy-start | bytes 1179652
  267.6 41.0 %reduce-scatter.5.cloned.1.call-start = ((), (), s32[]{:S(2)}) async-start(), calls=%async_computation.4 | async-start | bytes 393216 | tf_op jit(solution)/shard_map/reduce_scatter | solution.py:146
  269.5 39.1 %copy-start.17 = (f32[256]{0:T(256)S(1)}, f32[256]{0:T(256)}, u32[]{:S(2)}) copy-start(f32[256]{0:T(256)} %param.20) | copy-start | bytes 3076
  270.3 44.9 %copy-start.5 = (bf16[6,8,16,256]{3,1,2,0:T(8,128)(2,1)S(1)}, bf16[6,8,16,256]{3,1,2,0:T(8,128)(2,1)}, u32[]{:S(2)}) copy-start(bf16[6,8,16,256]{3,1,2,0:T(8,128)(2,1)} %copy.60) | copy-start | bytes 1179652
  271.1 44.8 %copy-start.6 = (bf16[16,256,48]{1,0,2:T(8,128)(2,1)S(1)}, bf16[16,256,48]{1,0,2:T(8,128)(2,1)}, u32[]{:S(2)}) copy-start(bf16[16,256,48]{1,0,2:T(8,128)(2,1)} %get-tuple-element.19) | copy-start | bytes 1179652
  309.5 24.5 %copy-start.4 = (bf16[4,64,256]{2,1,0:T(8,128)(2,1)}, bf16[4,64,256]{2,1,0:T(8,128)(2,1)S(1)}, u32[]{:S(2)}) copy-start(bf16[4,64,256]{2,1,0:T(8,128)(2,1)S(1)} %maximum_convert_fusion.2) | copy-start | bytes 393220
  309.6 6.5 %collective-permute-start.11 = (bf16[1,64,256]{2,1,0:T(8,128)(2,1)S(1)}, bf16[1,64,256]{2,1,0:T(8,128)(2,1)S(1)}, u32[]{:S(2)}, u32[]{:S(2)}) collective-permute-start(bf16[1,64,256]{2,1,0:T(8,128)(2,1)S(1)} %get-tuple-element.42), channel_id=1, source_target_pairs={{2,0},{4,2},{6,4},{8,6},{10,8},{12,10},{14,12},{16,14},{18,16},{20... | collective-permute-start | bytes 98312 | tf_op jit(solution)/shard_map/ppermute | solution.py:26
  312.2 4.0 %collective-permute-start.10 = (bf16[1,64,256]{2,1,0:T(8,128)(2,1)S(1)}, bf16[1,64,256]{2,1,0:T(8,128)(2,1)S(1)}, u32[]{:S(2)}, u32[]{:S(2)}) collective-permute-start(bf16[1,64,256]{2,1,0:T(8,128)(2,1)S(1)} %get-tuple-element.41), channel_id=1, source_target_pairs={{0,2},{2,4},{4,6},{6,8},{8,10},{10,12},{12,14},{14,16},{16,18},{18... | collective-permute-start | bytes 98312 | tf_op jit(solution)/shard_map/ppermute | solution.py:25
  316.2 17.4 %collective-permute-start.13 = (bf16[6,1,256]{2,1,0:T(2,128)(2,1)S(1)}, bf16[6,1,256]{2,1,0:T(2,128)(2,1)S(1)}, u32[]{:S(2)}, u32[]{:S(2)}) collective-permute-start(bf16[6,1,256]{2,1,0:T(2,128)(2,1)S(1)} %get-tuple-element.40), channel_id=1, source_target_pairs={{1,0},{3,2},{5,4},{7,6},{9,8},{11,10},{13,12},{15,14},{17,16},{19,... | collective-permute-start | bytes 9224 | tf_op jit(solution)/shard_map/ppermute | solution.py:26
  317.5 16.1 %collective-permute-start.12 = (bf16[6,1,256]{2,1,0:T(2,128)(2,1)S(1)}, bf16[6,1,256]{2,1,0:T(2,128)(2,1)S(1)}, u32[]{:S(2)}, u32[]{:S(2)}) collective-permute-start(bf16[6,1,256]{2,1,0:T(2,128)(2,1)S(1)} %get-tuple-element.39), channel_id=1, source_target_pairs={{0,1},{2,3},{4,5},{6,7},{8,9},{10,11},{12,13},{14,15},{16,17},{18,... | collective-permute-start | bytes 9224 | tf_op jit(solution)/shard_map/ppermute | solution.py:25
  (12 other events, 57.9 us)
Sparse Core Ops, SparseCore 0:
  10.2 146.0 all-gather.1
  267.8 26.1 reduce-scatter.2
  296.9 11.6 reduce-scatter.4
where the time goes:
time: 374 us; the launch traced here: 369 us
  local copies, waits for them, and re-layouts  93.5 us (25%)
  blocking collectives  76.3 us (20%)
  waiting for transfers between devices  70.9 us (19%)
  starting transfers between devices  63.7 us (17%)
  matrix products  39.3 us (11%)
  between operations  14.8 us (4%)
  other arithmetic  10.5 us (3%)
    psum x1, blocking collectives, on_device(): pooled = lax.psum(local_sum, 'rows') / map_total  72.2 us
    unnamed x98, local copies, waits for them, and re-layouts  63.3 us
    ppermute x10, waiting for transfers between devices, passed_along(): return lax.ppermute(block, axis, route)  35.9 us
    ppermute x10, starting transfers between devices, passed_along(): return lax.ppermute(block, axis, route)  30.6 us
    ppermute x4, starting transfers between devices, padded_2(): before = lax.ppermute(last, axis, up)  25.8 us
    reduce_scatter x1, waiting for transfers between devices, on_device(): lax.psum_scatter(partial_value.astype(jnp.bfloat16), 'chan', scatter_dime...  21.3 us
    dot_general x3, matrix products, on_device(): jnp.dot(matrix, weight_flat, preferred_element_type=jnp.float32)  20.5 us
    slice x1, local copies, waits for them, and re-layouts, on_device(): weight_flat = rate_all[rate_level].reshape(-1, rate_all.shape[3])  10.8 us
  transfers between devices with their start and end apart: 21, of which 8 were waited for; matrix products, arithmetic and copies ran while one was open for 14% of the time, Pallas kernels for 0%

commit v1 on v0

--- a/solution.py
+++ b/solution.py
@@ -1,6 +1,8 @@
 import jax
 import jax.numpy as jnp
 from jax import lax
+from jax.experimental import pallas as pl
+from jax.experimental.pallas import tpu as pltpu
 from jax.sharding import PartitionSpec as P
 
 RATE = 6
@@ -86,21 +88,374 @@
     return stacked.reshape(out_rows * out_cols, -1)
 
 
-def on_device(
-    features,
-    low_features,
-    w_one,
-    w_rate,
-    w_pool,
-    b_branch,
-    w_proj,
-    b_proj,
-    w_low,
-    b_low,
-    w_dec_up,
-    w_dec_low,
-    b_dec,
+F32 = jnp.float32
+BF16 = jnp.bfloat16
+MESH = pl.DeviceIdType.MESH
+
+
+def dot_t(lhs, rhs):
+    return lax.dot_general(lhs, rhs, (((1,), (1,)), ((), ())), preferred_element_type=F32)
+
+
+def pyramid_kernel(
+    geometry,
+    f_ref, own_ref, one_ref, pool_ref, branch_bias_ref, proj_ref, proj_bias_ref,
+    out_ref,
+    wbuf, shifted, sums, row_send, row_recv, merged, chan_recv, total, context, halo,
+    pool_send, pool_recv, pool_line,
+    gather_send, gather_recv, row_ssem, row_rsem, chan_ssem, chan_rsem, halo_ssem, halo_rsem,
+    pool_ssem, pool_rsem,
 ):
+    rows, lines, window, fine = geometry
+    strip, cols, depth = f_ref.shape
+    width = one_ref.shape[1]
+    pixels = strip * cols
+    me = lax.axis_index("rows")
+    chan = lax.axis_index("chan")
+    mine_z = me // 4
+    mine_y = (me // 2) % 2
+    core_peer = me + 1 - 2 * (me % 2)
+    y_peer = me + 2 - 4 * mine_y
+    chan_peer = 1 - chan
+    levels = own_ref.shape[0]
+    pending = []
+
+    def remote(src, dst, ssem, rsem, device):
+        return pltpu.make_async_remote_copy(
+            src_ref=src, dst_ref=dst, send_sem=ssem, recv_sem=rsem, device_id=device, device_id_type=MESH
+        )
+
+    def send(cond, copy):
+        if cond is None:
+            copy.start()
+        else:
+            pl.when(cond)(copy.start)
+        pending.append((cond, copy))
+
+    def arrive(cond, ref, rsem, ssem):
+        copy = remote(ref, ref, ssem, rsem, {"chan": chan_peer})
+        if cond is None:
+            copy.wait_recv()
+        else:
+            pl.when(cond)(copy.wait_recv)
+
+    row_recv[...] = jnp.zeros_like(row_recv)
+    wbuf[me] = own_ref[...]
+
+    barrier = pltpu.get_barrier_semaphore()
+    for step in range(1, rows):
+        pl.semaphore_signal(
+            barrier, inc=1, device_id={"rows": lax.rem(me + step, rows)}, device_id_type=MESH
+        )
+    pl.semaphore_signal(barrier, inc=1, device_id={"chan": chan_peer}, device_id_type=MESH)
+    pl.semaphore_wait(barrier, rows)
+
+    counter = [0]
+
+    def pass_shard(cond, source, level, target):
+        index = counter[0]
+        counter[0] += 1
+        slot = wbuf.at[source, level]
+        send(
+            cond,
+            remote(slot, slot, gather_send.at[index], gather_recv.at[level, source], {"rows": target}),
+        )
+
+    def shard_here(cond, source, level):
+        arrive(cond, wbuf.at[source, level], gather_recv.at[level, source], gather_send.at[0])
+
+    def both(one, other):
+        return other if one is None else one & other
+
+    order = list(range(levels))[::-1]
+    for level in order:
+        pass_shard(mine_z + 1 < lines, me, level, me + 4)
+        pass_shard(mine_z > 0, me, level, me - 4)
+        pass_shard(None, me, level, y_peer)
+        pass_shard(None, me, level, core_peer)
+
+    def flat():
+        return f_ref[...].reshape(pixels, depth)
+
+    local = jnp.zeros((8, depth), F32)
+    for row in range(strip):
+        block = f_ref[row].astype(F32).reshape(cols // 8, 8, depth)
+        local = local + jnp.sum(block, axis=0)
+    local = jnp.broadcast_to(jnp.sum(local, axis=0, keepdims=True), (8, depth))
+    pool_send[0] = jnp.dot(
+        local, pool_ref[...].astype(F32), precision=lax.Precision.HIGHEST, preferred_element_type=F32
+    )
+    peers = ({"chan": chan_peer}, {"rows": core_peer}, {"rows": y_peer})
+
+    def pool_round(turn):
+        send(
+            None,
+            remote(
+                pool_send.at[turn], pool_recv.at[turn], pool_ssem.at[turn], pool_rsem.at[turn], peers[turn]
+            ),
+        )
+
+    def pool_add(turn):
+        arrive(None, pool_recv.at[turn], pool_rsem.at[turn], pool_ssem.at[turn])
+        pool_send[turn + 1] = pool_send[turn] + pool_recv[turn]
+
+    def merge(slot, value):
+        merged[slot] = value.astype(BF16).reshape(strip, cols, width)
+        start = pl.multiple_of(chan_peer * (cols - window), 16)
+        send(
+            None,
+            remote(
+                merged.at[slot, :, pl.ds(start, window), :],
+                chan_recv.at[slot],
+                chan_ssem.at[slot],
+                chan_rsem.at[slot],
+                {"chan": chan_peer},
+            ),
+        )
+
+    def project(slot, first):
+        arrive(None, chan_recv.at[slot], chan_rsem.at[slot], chan_ssem.at[slot])
+        start = pl.multiple_of(chan * (cols - window), 16)
+        value = merged[slot, :, pl.ds(start, window), :].astype(F32) + chan_recv[slot].astype(F32)
+        value = jax.nn.relu(value + branch_bias_ref[slot : slot + 1, :].reshape(1, 1, width))
+        value = value.astype(BF16).reshape(strip * window, width)
+        term = jnp.dot(
+            value, proj_ref[slot * width : (slot + 1) * width, :], preferred_element_type=F32
+        )
+        if first:
+            total[...] = term
+        else:
+            total[...] += term
+
+    def shift_level(level):
+        spacing = RATE * (level + 1)
+        pos = lax.broadcasted_iota(jnp.int32, (cols, depth), 0)
+        for row in range(strip):
+            value = f_ref[row].astype(F32)
+            before = jnp.where(pos < spacing, 0.0, pltpu.roll(value, spacing, 0))
+            after = jnp.where(pos >= cols - spacing, 0.0, pltpu.roll(value, cols - spacing, 0))
+            shifted[level, 0, row] = before.astype(BF16)
+            shifted[level, 1, row] = after.astype(BF16)
+
+    pool_round(0)
+    merge(0, jnp.dot(flat(), one_ref[...], preferred_element_type=F32))
+    pool_add(0)
+    pool_round(1)
+    shift_level(order[0])
+    pool_add(1)
+    pool_round(2)
+    for level in order[1:]:
+        shift_level(level)
+    pool_add(2)
+    pool_line[mine_z] = pool_send[3]
+    for step in range(1, lines):
+        for at, sign in enumerate((1, -1)):
+            there = mine_z + sign * step
+            cond = (there >= 0) & (there < lines)
+            send(
+                cond,
+                remote(
+                    pool_send.at[3],
+                    pool_line.at[mine_z],
+                    pool_ssem.at[3 + 2 * (step - 1) + at],
+                    pool_rsem.at[3 + mine_z],
+                    {"rows": me + 4 * sign * step},
+                ),
+            )
+    project(0, True)
+
+    def gather_level(level):
+        for step in range(1, lines):
+            for sign in (-1, 1):
+                source = me + 4 * sign * step
+                here = (mine_z + sign * step >= 0) & (mine_z + sign * step < lines)
+                beyond = here & (mine_z - sign >= 0) & (mine_z - sign < lines)
+                shard_here(here, source, level)
+                pass_shard(beyond, source, level, me - 4 * sign)
+                pass_shard(here, source, level, y_peer)
+                pass_shard(here, source, level, core_peer)
+        for step in range(lines):
+            for sign in (-1, 1) if step else (1,):
+                source = y_peer + 4 * sign * step
+                here = (mine_z + sign * step >= 0) & (mine_z + sign * step < lines)
+                shard_here(here, source, level)
+                pass_shard(here, source, level, core_peer)
+        for line in range(lines):
+            for y in range(2):
+                shard_here(None, line * 4 + y * 2 + 1 - me % 2, level)
+
+    def row_copies(level):
+        hop, remain = divmod(RATE * (level + 1), strip)
+        found = []
+        if remain < strip:
+            found.append((0, hop, 0, remain, strip - remain))
+            found.append((1, -hop, remain, 0, strip - remain))
+        if remain > 0:
+            found.append((0, hop + 1, strip - remain, 0, remain))
+            found.append((1, -hop - 1, 0, strip - remain, remain))
+        return found
+
+    def compute_level(level):
+        spread = levels * 3
+
+        @pl.loop(0, 3)
+        def _(down):
+            value = None
+            for across in range(3):
+                weight = wbuf[:, level, 3 * down + across].reshape(width, depth)
+                side = f_ref[...] if across == 1 else shifted[level, across // 2]
+                term = dot_t(side.reshape(pixels, depth), weight)
+                value = term if value is None else value + term
+            sums[level, down] = value
+
+        for at, down in enumerate((0, 2)):
+            row_send[level, at] = sums[level, down].astype(BF16).reshape(strip, cols, width)
+        for index, (at, offset, first, into, count) in enumerate(row_copies(level)):
+            cond = (me + offset >= 0) & (me + offset < rows)
+            send(
+                cond,
+                remote(
+                    row_send.at[level, at, pl.ds(first, count)],
+                    row_recv.at[level, at, pl.ds(into, count)],
+                    row_ssem.at[level, index],
+                    row_rsem.at[level, index],
+                    {"rows": me + offset},
+                ),
+            )
+
+    def finish_level(level):
+        for index, (at, offset, first, into, count) in enumerate(row_copies(level)):
+            cond = (me - offset >= 0) & (me - offset < rows)
+            arrive(
+                cond, row_recv.at[level, at, pl.ds(into, count)], row_rsem.at[level, index], row_ssem.at[level, index]
+            )
+        value = sums[level, 1].reshape(strip, cols, width)
+        value = value + row_recv[level, 0].astype(F32) + row_recv[level, 1].astype(F32)
+        merge(level + 1, value)
+
+    for turn, level in enumerate(order):
+        gather_level(level)
+        compute_level(level)
+        if turn >= 1:
+            finish_level(order[turn - 1])
+        if turn >= 2:
+            project(order[turn - 2] + 1, False)
+
+    for step in range(1, lines):
+        for sign in (1, -1):
+            there = mine_z + sign * step
+            cond = (there >= 0) & (there < lines)
+            arrive(cond, pool_line.at[there], pool_rsem.at[3 + there], pool_ssem.at[0])
+    pooled = pool_line[0]
+    for line in range(1, lines):
+        pooled = pooled + pool_line[line]
+    pooled = pooled * (1.0 / (rows * pixels))
+    pooled = jax.nn.relu(pooled + branch_bias_ref[4:5, :]).astype(BF16)
+    constant = jnp.dot(pooled, proj_ref[4 * width :, :], preferred_element_type=F32)
+    constant = constant[0:1, :] + proj_bias_ref[...]
+
+    finish_level(order[-1])
+    for level in order[-2:]:
+        project(level + 1, False)
+
+    value = jax.nn.relu(total[...] + constant).astype(BF16).reshape(strip, window, width)
+    context[...] = value
+    out_ref[1 : strip + 1] = value
+    for at, (row, offset) in enumerate(((0, -1), (strip - 1, 1))):
+        cond = (me + offset >= 0) & (me + offset < rows)
+        send(
+            cond,
+            remote(context.at[row], halo.at[at], halo_ssem.at[at], halo_rsem.at[at], {"rows": me + offset}),
+        )
+    for at, (row, offset) in enumerate(((0, -1), (strip - 1, 1))):
+        place = strip + 1 if at == 0 else 0
+        edge = strip - 1 if at == 0 else 0
+        cond = (me - offset >= 0) & (me - offset < rows)
+        arrive(cond, halo.at[at], halo_rsem.at[at], halo_ssem.at[at])
+
+        @pl.when(cond)
+        def _():
+            out_ref[place] = halo[at]
+
+        @pl.when(jnp.logical_not(cond))
+        def _():
+            out_ref[place] = context[edge]
+
+    for cond, copy in pending:
+        if cond is None:
+            copy.wait_send()
+        else:
+            pl.when(cond)(copy.wait_send)
+
+
+def pyramid(features, w_one, w_rate, w_pool, b_branch, w_proj, b_proj):
+    strip, cols, depth = features.shape
+    levels, taps, shard = w_rate.shape[0], w_rate.shape[1], w_rate.shape[3]
+    width = w_one.shape[1]
+    rows = lax.axis_size("rows")
+    lines = rows // 4
+    window = cols // 2 + 16
+    pixels = strip * cols
+    own = jnp.swapaxes(w_rate, 2, 3)
+    sends = levels * (4 + 2 * 3 * (lines - 1) + 2 * lines)
+    dma = pltpu.SemaphoreType.DMA
+    vmem = pl.BlockSpec(memory_space=pltpu.VMEM)
+    return pl.pallas_call(
+        lambda *refs: pyramid_kernel((rows, lines, window, None), *refs),
+        out_shape=jax.ShapeDtypeStruct((strip + 2, window, width), BF16),
+        in_specs=[vmem] * 7,
+        out_specs=vmem,
+        scratch_shapes=[
+            pltpu.VMEM((rows, levels, taps, shard, depth), BF16),
+            pltpu.VMEM((levels, 2, strip, cols, depth), BF16),
+            pltpu.VMEM((levels, 3, pixels, width), F32),
+            pltpu.VMEM((levels, 2, strip, cols, width), BF16),
+            pltpu.VMEM((levels, 2, strip, cols, width), BF16),
+            pltpu.VMEM((levels + 1, strip, cols, width), BF16),
+            pltpu.VMEM((levels + 1, strip, window, width), BF16),
+            pltpu.VMEM((strip * window, width), F32),
+            pltpu.VMEM((strip, window, width), BF16),
+            pltpu.VMEM((2, window, width), BF16),
+            pltpu.VMEM((4, 8, width), F32),
+            pltpu.VMEM((3, 8, width), F32),
+            pltpu.VMEM((lines, 8, width), F32),
+            dma((sends,)),
+            dma((levels, rows)),
+            dma((levels, 4)),
+            dma((levels, 4)),
+            dma((levels + 1,)),
+            dma((levels + 1,)),
+            dma((2,)),
+            dma((2,)),
+            dma((3 + 2 * lines,)),
+            dma((3 + lines,)),
+        ],
+        compiler_params=pltpu.CompilerParams(
+            collective_id=0, has_side_effects=True, vmem_limit_bytes=56 * 1024 * 1024
+        ),
+        cost_estimate=pl.CostEstimate(
+            flops=2 * pixels * depth * width * (levels * taps + 1),
+            bytes_accessed=2 * levels * taps * depth * width,
+            transcendentals=0,
+        ),
+    )(features, own, w_one, w_pool, b_branch, w_proj, b_proj[None, :])
+
+
+def context_by_kernel(features, w_one, w_rate, w_pool, b_branch, w_proj, b_proj):
+    cols = features.shape[1]
+    chan_index = lax.axis_index("chan")
+    padded = pyramid(features, w_one, w_rate, w_pool, b_branch, w_proj, b_proj)
+    half = cols // 2
+    context = jnp.where(chan_index == 0, padded[1:-1, :half], padded[1:-1, 16:])
+    coarse = jnp.where(
+        chan_index == 0,
+        jnp.concatenate([padded[:, :1], padded[:, : half + 1]], axis=1),
+        jnp.concatenate([padded[:, 15:], padded[:, -1:]], axis=1),
+    )
+    return context, coarse
+
+
+def context_by_collectives(features, w_one, w_rate, w_pool, b_branch, w_proj, b_proj):
     strip_rows, map_cols, group_in = features.shape
     branch_width = w_one.shape[1]
     pixel_count = strip_rows * map_cols
@@ -147,6 +502,39 @@
         partial_terms.astype(jnp.bfloat16), "chan", scatter_dimension=1, tiled=True
     ).astype(jnp.float32)
     context = jax.nn.relu(projected + pool_term + b_proj).astype(jnp.bfloat16)
+    coarse = padded_2(context, (("rows", 0), ("chan", 1)), 1)
+    coarse = edge_copy(coarse, rows_index, rows_count, chan_index, chan_count)
+    return context, coarse
+
+
+def on_device(
+    features,
+    low_features,
+    w_one,
+    w_rate,
+    w_pool,
+    b_branch,
+    w_proj,
+    b_proj,
+    w_low,
+    b_low,
+    w_dec_up,
+    w_dec_low,
+    b_dec,
+):
+    rows_index = lax.axis_index("rows")
+    rows_count = lax.axis_size("rows")
+    chan_index = lax.axis_index("chan")
+    chan_count = lax.axis_size("chan")
+    fits = (
+        chan_count == 2
+        and rows_count % 4 == 0
+        and w_rate.shape[3] % 16 == 0
+        and features.shape[1] % 32 == 0
+        and features.shape[2] % 128 == 0
+    )
+    make_context = context_by_kernel if fits else context_by_collectives
+    context, coarse = make_context(features, w_one, w_rate, w_pool, b_branch, w_proj, b_proj)
     tile_rows_count = context.shape[0]
     tile_cols_count = context.shape[1]
     fine_rows, fine_cols = (low_features.shape[0], low_features.shape[1])
@@ -155,8 +543,7 @@
         jnp.dot(low_flat, w_low, preferred_element_type=jnp.float32) + b_low
     ).astype(jnp.bfloat16)
     low_mapped = low_mapped.reshape(fine_rows, fine_cols, -1)
-    coarse = padded_2(context, (("rows", 0), ("chan", 1)), 1)
-    coarse = edge_copy(coarse, rows_index, rows_count, chan_index, chan_count).astype(jnp.float32)
+    coarse = coarse.astype(jnp.float32)
     upsampled = blend_axis(coarse, 0)[1 : 4 * tile_rows_count + 3]
     upsampled = blend_axis(upsampled, 1)[:, 1 : 4 * tile_cols_count + 3]
     ext_rows, ext_cols = (upsampled.shape[0], upsampled.shape[1])

time: 374 us -> 189 us (0.51)
  Pallas kernels: 0 us -> 134 us
  blocking collectives: 76.3 us -> 0 us
  local copies, waits for them, and re-layouts: 93.5 us -> 20.3 us
  waiting for transfers between devices: 70.9 us -> 2.85 us
  starting transfers between devices: 63.7 us -> 12 us
  matrix products: 39.3 us -> 9.74 us
  between operations: 14.8 us -> 1.04 us
    pallas_call x0 -> x1, Pallas kernels: none -> 134 us  [pyramid(): pl.pallas_call(lambda *refs: pyramid_kernel((rows, lines, window, None),...]
    psum x2 -> x0, blocking collectives: 76.3 us -> none  [the longest x1 72.2 us: on_device(): pooled = lax.psum(local_sum, 'rows') / map_total]
    unnamed x98 -> x35, local copies, waits for them, and re-layouts: 63.3 us -> 8.44 us
    ppermute x10 -> x0, waiting for transfers between devices: 35.9 us -> none  [passed_along(): return lax.ppermute(block, axis, route)]
    reduce_scatter x2 -> x0, waiting for transfers between devices: 32 us -> none  [the longest x1 21.3 us: on_device(): lax.psum_scatter(partial_value.astype(jnp.bfloat16), 'chan', scatter_dime...]
    ppermute x10 -> x0, starting transfers between devices: 30.6 us -> none  [passed_along(): return lax.ppermute(block, axis, route)]
    dot_general x7 -> x0, matrix products: 27.3 us -> none  [the longest x3 20.5 us: on_device(): jnp.dot(matrix, weight_flat, preferred_element_type=jnp.float32)]
    ppermute x4 -> x2, starting transfers between devices: 25.8 us -> 8.73 us  [padded_2(): before = lax.ppermute(last, axis, up)]
  transfers between devices with their start and end apart: 21 -> 4, of which waited for: 8 -> 2; matrix products, arithmetic and copies ran while one was open for 14% -> 14% of each run, Pallas kernels for 0% -> 71%
where the time goes in v1:
time: 189 us; the launch traced here: 187 us
  Pallas kernels  134 us (71%)
  local copies, waits for them, and re-layouts  20.3 us (11%)
  starting transfers between devices  12 us (6%)
  matrix products  9.74 us (5%)
  other arithmetic  7.57 us (4%)
  waiting for transfers between devices  2.85 us (2%)
    pallas_call x1, Pallas kernels, pyramid(): pl.pallas_call(lambda *refs: pyramid_kernel((rows, lines, window, None),...  134 us
    ppermute x2, starting transfers between devices, padded_2(): before = lax.ppermute(last, axis, up)  8.73 us
    unnamed x35, local copies, waits for them, and re-layouts  8.44 us
    dot_general x1, matrix products, on_device(): jnp.dot(up_taps, w_dec_up.reshape(-1, w_dec_up.shape[2]), preferred_eleme...  5.59 us
    reshape x1, local copies, waits for them, and re-layouts, blend_axis(): return blended.reshape(target)  5.05 us
  transfers between devices with their start and end apart: 4, of which 2 were waited for; matrix products, arithmetic and copies ran while one was open for 14% of the time, Pallas kernels for 71%

profile of v1, /device:TPU:1, one launch (start us, length us, event | category | flops | bytes accessed | tf_op | source)
XLA Modules:
  0.0 187.3 jit_solution(4206449760235178869)
XLA Ops:
  0.6 1.6 copy-done
  2.2 1.5 fusion.5
  3.7 2.0 %collective-permute-start.1 = (bf16[1,256,48]{1,2,0:T(8,128)(2,1)S(1)}, bf16[1,256,48]{1,2,0:T(8,128)(2,1)S(1)}, u32[]{:S(2)}, u32[]{:S(2)}) collective-permute-start(bf16[1,256,48]{1,2,0:T(8,128)(2,1)S(1)} %get-tuple-element.23), channel_id=1, source_target_pairs={{2,0},{4,2},{6,4},{8,6},{10,8},{12,10},{14,12},{16,14},{18,16},{20... | collective-permute-start | bytes 73736 | tf_op jit(solution)/shard_map/ppermute | solution.py:28
  5.7 4.5 %collective-permute-start = (bf16[1,256,48]{1,2,0:T(8,128)(2,1)S(1)}, bf16[1,256,48]{1,2,0:T(8,128)(2,1)S(1)}, u32[]{:S(2)}, u32[]{:S(2)}) collective-permute-start(bf16[1,256,48]{1,2,0:T(8,128)(2,1)S(1)} %get-tuple-element.22), channel_id=1, source_target_pairs={{0,2},{2,4},{4,6},{6,8},{8,10},{10,12},{12,14},{14,16},{16,18},{18... | collective-permute-start | bytes 73736 | tf_op jit(solution)/shard_map/ppermute | solution.py:27
  10.2 133.9 %shard_map.140 = bf16[6,80,256]{2,1,0:T(8,128)(2,1)} custom-call(bf16[4,128,1024]{2,1,0:T(8,128)(2,1)} %refs_0_.1, bf16[3,9,16,1024]{3,2,1,0:T(8,128)(2,1)} %bitcast.94, bf16[1024,256]{1,0:T(8,128)(2,1)} %refs_2_.1, bf16[1024,256]{1,0:T(8,128)(2,1)} %refs_3_.1, f32[5,256]{1,0:T(8,128)} %refs_4_.1, bf16[1280,256]{1,0:T(8,128)(2,1)} %refs_5_.1, f32[1,256]{1,0:T(1,128)} %bitcast.96), custom_call_target="tpu_custom_call" | custom-call | flops 7516192768 | bytes 14155776 | tf_op jit(solution)/shard_map/pallas_call | solution.py:403
  144.1 1.1 fusion.12
  145.2 0.8 fusion.13
  146.5 0.7 add_bitcast_fusion.3
  147.2 0.3 pad_maximum_fusion
  147.6 2.7 %copy.28 = bf16[18,65,4,256]{3,2,1,0:T(4,128)(2,1)} copy(bf16[18,65,4,256]{3,1,0,2:T(8,128)(2,1)S(1)} %pad_maximum_fusion) | data formatting | bytes 4792320 | tf_op jit(solution)/shard_map/stack | solution.py:64
  150.3 5.0 %reshape.121 = bf16[18,260,256]{2,1,0:T(8,128)(2,1)} reshape(bf16[18,65,4,256]{3,2,1,0:T(4,128)(2,1)} %copy.28) | data formatting | bytes 4792320 | tf_op jit(solution)/shard_map/reshape | solution.py:69
  155.4 3.3 %fusion.3 = bf16[18,258,256]{2,1,0:T(8,128)(2,1)S(1)} fusion(bf16[18,260,256]{2,1,0:T(8,128)(2,1)} %reshape.121, pred[18,258]{1,0:T(8,128)(4,1)S(1)} %and_and_fusion), kind=kLoop, calls=%fused_computation.6 | loop fusion | flops 1188864 | bytes 4760100 | tf_op jit(solution)/shard_map/convert_element_type | solution.py:560
  158.9 0.8 slice_dynamic-update-slice_fusion.7
  159.7 0.8 slice_dynamic-update-slice_fusion.6
  160.5 0.2 slice_dynamic-update-slice_fusion.5
  160.7 0.8 slice_dynamic-update-slice_fusion.4
  161.5 0.8 slice_dynamic-update-slice_fusion.3
  162.5 0.8 slice_dynamic-update-slice_fusion.1
  163.3 0.8 slice_dynamic-update-slice_fusion
  164.1 0.5 copy-done.2
  164.6 5.6 %fusion.14 = f32[4096,256]{1,0:T(8,128)S(1)} fusion(bf16[4096,2304]{1,0:T(8,128)(2,1)S(1)} %bitcast.92, bf16[2304,256]{1,0:T(8,128)(2,1)S(1)} %bitcast.93), kind=kOutput, calls=%fused_computation.58 | convolution fusion | flops 4831838208 | bytes 24248320 | tf_op jit(solution)/shard_map/dot_general | solution.py:564
  170.2 0.7 slice_select_fusion.1
  171.1 0.3 pad_maximum_fusion.3
  171.6 1.3 collective-permute-start.3
  172.9 4.2 %collective-permute-start.2 = (bf16[18,1,48]{1,0,2:T(8,128)(2,1)S(1)}, bf16[18,1,48]{1,0,2:T(8,128)(2,1)S(1)}, u32[]{:S(2)}, u32[]{:S(2)}) collective-permute-start(bf16[18,1,48]{1,0,2:T(8,128)(2,1)S(1)} %get-tuple-element.13), channel_id=1, source_target_pairs={{0,1},{2,3},{4,5},{6,7},{8,9},{10,11},{12,13},{14,15},{16,17},{18,... | collective-permute-start | bytes 5192 | tf_op jit(solution)/shard_map/ppermute | solution.py:27
  177.1 0.4 pad_maximum_fusion.4
  177.8 1.3 collective-permute-done.3
  179.0 1.6 collective-permute-done.2
  180.6 1.3 pad_maximum_fusion.2
  181.9 1.0 fusion.9
  184.1 0.5 copy-done.3
  184.6 2.7 %fusion.2 = bf16[4096,256]{1,0:T(8,128)(2,1)} fusion(f32[4096,256]{1,0:T(8,128)S(1)} %fusion.14, bf16[4096,432]{0,1:T(8,128)(2,1)S(1)} %constant_dynamic-update-slice_fusion, bf16[432,256]{1,0:T(8,128)(2,1)S(1)} %bitcast.95, f32[256]{0:T(256)S(1)} %copy-done.4), kind=kOutput, calls=%fused_computation.4 | convolution fusion | flops 910163968 | bytes 10052608 | tf_op jit(solution)/shard_map/dot_general | solution.py:567
  (40 shorter events, 2.6 us)
Async XLA Ops:
  0.6 1.6 copy-start
  3.7 167.2 %collective-permute-start.1 = (bf16[1,256,48]{1,2,0:T(8,128)(2,1)S(1)}, bf16[1,256,48]{1,2,0:T(8,128)(2,1)S(1)}, u32[]{:S(2)}, u32[]{:S(2)}) collective-permute-start(bf16[1,256,48]{1,2,0:T(8,128)(2,1)S(1)} %get-tuple-element.23), channel_id=1, source_target_pairs={{2,0},{4,2},{6,4},{8,6},{10,8},{12,10},{14,12},{16,14},{18,16},{20... | collective-permute-start | bytes 73736 | tf_op jit(solution)/shard_map/ppermute | solution.py:28
  5.7 165.3 %collective-permute-start = (bf16[1,256,48]{1,2,0:T(8,128)(2,1)S(1)}, bf16[1,256,48]{1,2,0:T(8,128)(2,1)S(1)}, u32[]{:S(2)}, u32[]{:S(2)}) collective-permute-start(bf16[1,256,48]{1,2,0:T(8,128)(2,1)S(1)} %get-tuple-element.22), channel_id=1, source_target_pairs={{0,2},{2,4},{4,6},{6,8},{8,10},{10,12},{12,14},{14,16},{16,18},{18... | collective-permute-start | bytes 73736 | tf_op jit(solution)/shard_map/ppermute | solution.py:27
  163.3 1.3 copy-start.2
  164.6 5.6 %copy-start.1 = (bf16[6,80,256]{2,1,0:T(8,128)(2,1)S(1)}, bf16[6,80,256]{2,1,0:T(8,128)(2,1)}, u32[]{:S(2)}) copy-start(bf16[6,80,256]{2,1,0:T(8,128)(2,1)} %shard_map.140) | copy-start | bytes 737284
  171.6 7.5 %collective-permute-start.3 = (bf16[18,1,48]{1,0,2:T(8,128)(2,1)S(1)}, bf16[18,1,48]{1,0,2:T(8,128)(2,1)S(1)}, u32[]{:S(2)}, u32[]{:S(2)}) collective-permute-start(bf16[18,1,48]{1,0,2:T(8,128)(2,1)S(1)} %get-tuple-element.12), channel_id=1, source_target_pairs={{1,0},{3,2},{5,4},{7,6},{9,8},{11,10},{13,12},{15,14},{17,16},{19,... | collective-permute-start | bytes 5192 | tf_op jit(solution)/shard_map/ppermute | solution.py:28
  172.9 7.8 %collective-permute-start.2 = (bf16[18,1,48]{1,0,2:T(8,128)(2,1)S(1)}, bf16[18,1,48]{1,0,2:T(8,128)(2,1)S(1)}, u32[]{:S(2)}, u32[]{:S(2)}) collective-permute-start(bf16[18,1,48]{1,0,2:T(8,128)(2,1)S(1)} %get-tuple-element.13), channel_id=1, source_target_pairs={{0,1},{2,3},{4,5},{6,7},{8,9},{10,11},{12,13},{14,15},{16,17},{18,... | collective-permute-start | bytes 5192 | tf_op jit(solution)/shard_map/ppermute | solution.py:27
  183.7 0.9 copy-start.3
  183.7 0.9 copy-start.4

commit v2 on v1

--- a/solution.py
+++ b/solution.py
@@ -100,13 +100,17 @@
 def pyramid_kernel(
     geometry,
     f_ref, own_ref, one_ref, pool_ref, branch_bias_ref, proj_ref, proj_bias_ref,
-    out_ref,
+    low_ref, low_weight_ref, low_bias_ref,
+    out_ref, low_out_ref,
     wbuf, shifted, sums, row_send, row_recv, merged, chan_recv, total, context, halo,
     pool_send, pool_recv, pool_line,
     gather_send, gather_recv, row_ssem, row_rsem, chan_ssem, chan_rsem, halo_ssem, halo_rsem,
     pool_ssem, pool_rsem,
+    low_edge, low_send, low_recv, low_rows_send, low_rows_recv, low_ssem, low_rsem,
 ):
-    rows, lines, window, fine = geometry
+    rows, lines, window, low_width = geometry
+    fine_rows, fine_cols, low_depth = low_ref.shape
+    packed = low_weight_ref.shape[1]
     strip, cols, depth = f_ref.shape
     width = one_ref.shape[1]
     pixels = strip * cols
@@ -140,6 +144,7 @@
             pl.when(cond)(copy.wait_recv)
 
     row_recv[...] = jnp.zeros_like(row_recv)
+    low_rows_recv[...] = jnp.zeros_like(low_rows_recv)
     wbuf[me] = own_ref[...]
 
     barrier = pltpu.get_barrier_semaphore()
@@ -237,6 +242,23 @@
             shifted[level, 0, row] = before.astype(BF16)
             shifted[level, 1, row] = after.astype(BF16)
 
+    def mapped_low(value):
+        return jax.nn.relu(
+            jnp.dot(value, low_weight_ref[...], preferred_element_type=F32) + low_bias_ref[...]
+        )
+
+    @pl.loop(0, fine_rows)
+    def _(row):
+        first = low_ref[row, 0:16, :].astype(F32)
+        last = low_ref[row, fine_cols - 16 : fine_cols, :].astype(F32)
+        low_edge[pl.ds(row, 1), :] = jnp.where(chan == 0, last[15:16], first[0:1])
+
+    low_send[...] = mapped_low(low_edge[...].astype(BF16))
+    send(
+        None,
+        remote(low_send, low_recv, low_ssem.at[0], low_rsem.at[0], {"chan": chan_peer}),
+    )
+
     pool_round(0)
     merge(0, jnp.dot(flat(), one_ref[...], preferred_element_type=F32))
     pool_add(0)
@@ -244,6 +266,35 @@
     shift_level(order[0])
     pool_add(1)
     pool_round(2)
+
+    arrive(None, low_recv, low_rsem.at[0], low_ssem.at[0])
+
+    @pl.loop(0, fine_rows)
+    def _(row):
+        value = mapped_low(low_ref[row])
+        pos = lax.broadcasted_iota(jnp.int32, (fine_cols, packed), 0)
+        lane = lax.broadcasted_iota(jnp.int32, (fine_cols, packed), 1)
+        outer = low_recv[pl.ds(row, 1), :]
+        left = jnp.where(chan == 0, 0.0, outer)
+        right = jnp.where(chan == 0, outer, 0.0)
+        before = jnp.where(pos == 0, left, pltpu.roll(value, 1, 0))
+        after = jnp.where(pos == fine_cols - 1, right, pltpu.roll(value, fine_cols - 1, 0))
+        value = jnp.where(lane < low_width, before, jnp.where(lane < 2 * low_width, value, after))
+        low_out_ref[row + 1] = value.astype(BF16)
+
+    low_rows_send[0] = low_out_ref[1]
+    low_rows_send[1] = low_out_ref[fine_rows]
+    for at, offset in enumerate((-1, 1)):
+        send(
+            (me + offset >= 0) & (me + offset < rows),
+            remote(
+                low_rows_send.at[at],
+                low_rows_recv.at[at],
+                low_ssem.at[1 + at],
+                low_rsem.at[1 + at],
+                {"rows": me + offset},
+            ),
+        )
     for level in order[1:]:
         shift_level(level)
     pool_add(2)
@@ -341,6 +392,11 @@
         if turn >= 2:
             project(order[turn - 2] + 1, False)
 
+    for at, (offset, place) in enumerate(((-1, fine_rows + 1), (1, 0))):
+        cond = (me - offset >= 0) & (me - offset < rows)
+        arrive(cond, low_rows_recv.at[at], low_rsem.at[1 + at], low_ssem.at[1 + at])
+        low_out_ref[place] = low_rows_recv[at]
+
     for step in range(1, lines):
         for sign in (1, -1):
             there = mine_z + sign * step
@@ -388,7 +444,7 @@
             pl.when(cond)(copy.wait_send)
 
 
-def pyramid(features, w_one, w_rate, w_pool, b_branch, w_proj, b_proj):
+def pyramid(features, w_one, w_rate, w_pool, b_branch, w_proj, b_proj, low_features, w_low, b_low):
     strip, cols, depth = features.shape
     levels, taps, shard = w_rate.shape[0], w_rate.shape[1], w_rate.shape[3]
     width = w_one.shape[1]
@@ -398,13 +454,22 @@
     pixels = strip * cols
     own = jnp.swapaxes(w_rate, 2, 3)
     sends = levels * (4 + 2 * 3 * (lines - 1) + 2 * lines)
+    fine_rows, fine_cols, low_depth = low_features.shape
+    low_width = w_low.shape[1]
+    packed = pl.cdiv(3 * low_width, 128) * 128
+    rest = packed - 3 * low_width
+    low_weight = jnp.pad(jnp.concatenate([w_low] * 3, axis=1), ((0, 0), (0, rest)))
+    low_bias = jnp.pad(jnp.concatenate([b_low] * 3), (0, rest))[None, :]
     dma = pltpu.SemaphoreType.DMA
     vmem = pl.BlockSpec(memory_space=pltpu.VMEM)
     return pl.pallas_call(
-        lambda *refs: pyramid_kernel((rows, lines, window, None), *refs),
-        out_shape=jax.ShapeDtypeStruct((strip + 2, window, width), BF16),
-        in_specs=[vmem] * 7,
-        out_specs=vmem,
+        lambda *refs: pyramid_kernel((rows, lines, window, low_width), *refs),
+        out_shape=(
+            jax.ShapeDtypeStruct((strip + 2, window, width), BF16),
+            jax.ShapeDtypeStruct((fine_rows + 2, fine_cols, packed), BF16),
+        ),
+        in_specs=[vmem] * 10,
+        out_specs=(vmem, vmem),
         scratch_shapes=[
             pltpu.VMEM((rows, levels, taps, shard, depth), BF16),
             pltpu.VMEM((levels, 2, strip, cols, depth), BF16),
@@ -429,6 +494,13 @@
             dma((2,)),
             dma((3 + 2 * lines,)),
             dma((3 + lines,)),
+            pltpu.VMEM((fine_rows, low_depth), F32),
+            pltpu.VMEM((fine_rows, packed), F32),
+            pltpu.VMEM((fine_rows, packed), F32),
+            pltpu.VMEM((2, fine_cols, packed), BF16),
+            pltpu.VMEM((2, fine_cols, packed), BF16),
+            dma((3,)),
+            dma((3,)),
         ],
         compiler_params=pltpu.CompilerParams(
             collective_id=0, has_side_effects=True, vmem_limit_bytes=56 * 1024 * 1024
@@ -438,21 +510,103 @@
             bytes_accessed=2 * levels * taps * depth * width,
             transcendentals=0,
         ),
-    )(features, own, w_one, w_pool, b_branch, w_proj, b_proj[None, :])
-
-
-def context_by_kernel(features, w_one, w_rate, w_pool, b_branch, w_proj, b_proj):
-    cols = features.shape[1]
+    )(
+        features, own, w_one, w_pool, b_branch, w_proj, b_proj[None, :],
+        low_features, low_weight, low_bias,
+    )
+
+
+def decoder_kernel(
+    strip, coarse_ref, low_ref, blend_ref, up_weight_ref, low_weight_ref, bias_ref, out_ref, fine
+):
+    at = pl.program_id(0)
+    me = lax.axis_index("rows")
+    rows = lax.axis_size("rows")
+    block, fine_cols, width = out_ref.shape
+    fine_rows = fine.shape[0] - 2
+    window, depth = coarse_ref.shape[1], coarse_ref.shape[2]
+
+    @pl.when(at == 0)
+    def _():
+        for row in range(fine_rows + 2):
+            pair, phase = divmod(row + 1, 4)
+            source = coarse_ref[pair : pair + 2].reshape(2 * window, depth)
+            for across in range(3):
+                value = jnp.dot(
+                    blend_ref[phase, across * fine_cols : (across + 1) * fine_cols, :],
+                    source,
+                    preferred_element_type=F32,
+                )
+                if row == 0:
+                    value = jnp.where(me == 0, 0.0, value)
+                if row == fine_rows + 1:
+                    value = jnp.where(me == rows - 1, 0.0, value)
+                fine[row, :, across * depth : (across + 1) * depth] = value.astype(BF16)
+
+    total = None
+    for down in range(3):
+        up = fine[pl.ds(at * block + down, block)].reshape(block * fine_cols, 3 * depth)
+        low = low_ref[pl.ds(at * block + down, block)].reshape(block * fine_cols, low_ref.shape[2])
+        term = jnp.dot(up, up_weight_ref[down], preferred_element_type=F32)
+        term = term + jnp.dot(low, low_weight_ref[down], preferred_element_type=F32)
+        total = term if total is None else total + term
+    total = jax.nn.relu(total + bias_ref[...])
+    out_ref[...] = total.astype(BF16).reshape(block, fine_cols, width)
+
+
+def blend_matrices(half, window, chan_index):
+    fine_cols = 4 * half
+    shape = (4, 3, fine_cols, 2, window)
+    phase, across, pos, lower, col = (lax.broadcasted_iota(jnp.int32, shape, d) for d in range(5))
+    place = pos + across - 1
+    pair, col_phase = (place + 2) // 4, (place + 2) % 4
+    first = jnp.clip(chan_index * half + pair - 1, 0, 2 * half - 1) - chan_index * (2 * half - window)
+    second = jnp.clip(chan_index * half + pair, 0, 2 * half - 1) - chan_index * (2 * half - window)
+    col_upper = 0.875 - 0.25 * col_phase.astype(F32)
+    factor = jnp.where(col == first, col_upper, 0.0) + jnp.where(col == second, 1.0 - col_upper, 0.0)
+    row_upper = 0.875 - 0.25 * phase.astype(F32)
+    factor = factor * jnp.where(lower == 0, row_upper, 1.0 - row_upper)
+    whole = chan_index * fine_cols + place
+    factor = jnp.where((whole >= 0) & (whole < 2 * fine_cols), factor, 0.0)
+    return factor.astype(BF16).reshape(4, 3 * fine_cols, 2 * window)
+
+
+def whole_by_kernels(
+    features, low_features, w_one, w_rate, w_pool, b_branch, w_proj, b_proj, w_low, b_low,
+    w_dec_up, w_dec_low, b_dec,
+):
+    strip, cols = features.shape[0], features.shape[1]
+    fine_rows, fine_cols = low_features.shape[0], low_features.shape[1]
+    depth, width = w_dec_up.shape[1], w_dec_up.shape[2]
     chan_index = lax.axis_index("chan")
-    padded = pyramid(features, w_one, w_rate, w_pool, b_branch, w_proj, b_proj)
     half = cols // 2
-    context = jnp.where(chan_index == 0, padded[1:-1, :half], padded[1:-1, 16:])
-    coarse = jnp.where(
-        chan_index == 0,
-        jnp.concatenate([padded[:, :1], padded[:, : half + 1]], axis=1),
-        jnp.concatenate([padded[:, 15:], padded[:, -1:]], axis=1),
-    )
-    return context, coarse
+    padded, low_packed = pyramid(
+        features, w_one, w_rate, w_pool, b_branch, w_proj, b_proj, low_features, w_low, b_low
+    )
+    window, packed = padded.shape[1], low_packed.shape[2]
+    context = jnp.where(chan_index == 0, padded[1:-1, :half], padded[1:-1, window - half :])
+    up_weight = w_dec_up.reshape(3, 3 * depth, width)
+    low_weight = w_dec_low.reshape(3, -1, width)
+    low_weight = jnp.pad(low_weight, ((0, 0), (0, packed - low_weight.shape[1]), (0, 0)))
+    blend = blend_matrices(half, window, chan_index)
+    whole = pl.BlockSpec(memory_space=pltpu.VMEM)
+    block = 4
+    pixels = fine_rows * fine_cols
+    decoded = pl.pallas_call(
+        lambda *refs: decoder_kernel(strip, *refs),
+        out_shape=jax.ShapeDtypeStruct((fine_rows, fine_cols, width), BF16),
+        grid=(fine_rows // block,),
+        in_specs=[whole] * 6,
+        out_specs=pl.BlockSpec((block, fine_cols, width), lambda i: (i, 0, 0)),
+        scratch_shapes=[pltpu.VMEM((fine_rows + 2, fine_cols, 3 * depth), BF16)],
+        compiler_params=pltpu.CompilerParams(vmem_limit_bytes=48 * 1024 * 1024),
+        cost_estimate=pl.CostEstimate(
+            flops=2 * pixels * width * (9 * depth + 3 * packed),
+            bytes_accessed=2 * pixels * (width + packed),
+            transcendentals=0,
+        ),
+    )(padded, low_packed, blend, up_weight, low_weight, b_dec[None, :])
+    return context, decoded
 
 
 def context_by_collectives(features, w_one, w_rate, w_pool, b_branch, w_proj, b_proj):
@@ -532,9 +686,19 @@
         and w_rate.shape[3] % 16 == 0
         and features.shape[1] % 32 == 0
         and features.shape[2] % 128 == 0
-    )
-    make_context = context_by_kernel if fits else context_by_collectives
-    context, coarse = make_context(features, w_one, w_rate, w_pool, b_branch, w_proj, b_proj)
+        and features.shape[0] % 2 == 0
+        and low_features.shape[0] == 4 * features.shape[0]
+        and low_features.shape[0] % 16 == 0
+        and 2 * low_features.shape[1] == 4 * features.shape[1]
+    )
+    if fits:
+        return whole_by_kernels(
+            features, low_features, w_one, w_rate, w_pool, b_branch, w_proj, b_proj, w_low, b_low,
+            w_dec_up, w_dec_low, b_dec,
+        )
+    context, coarse = context_by_collectives(
+        features, w_one, w_rate, w_pool, b_branch, w_proj, b_proj
+    )
     tile_rows_count = context.shape[0]
     tile_cols_count = context.shape[1]
     fine_rows, fine_cols = (low_features.shape[0], low_features.shape[1])

time: 189 us -> 156 us (0.83)
  local copies, waits for them, and re-layouts: 20.3 us -> 4.71 us
  starting transfers between devices: 12 us -> 0 us
  Pallas kernels: 134 us -> 145 us
  matrix products: 9.74 us -> 0 us
  other arithmetic: 7.57 us -> 4.36 us
  waiting for transfers between devices: 2.85 us -> 0 us
    ppermute x4 -> x0, starting transfers between devices: 12 us -> none  [the longest x2 8.73 us: padded_2(): before = lax.ppermute(last, axis, up)]
    pallas_call x1 -> x2, Pallas kernels: 134 us -> 145 us  [the longest x1 135 us: pyramid(): pl.pallas_call(lambda *refs: pyramid_kernel((rows, lines, window, low_wid...]
    dot_general x3 -> x0, matrix products: 9.74 us -> none  [the longest x1 5.59 us: on_device(): jnp.dot(up_taps, w_dec_up.reshape(-1, w_dec_up.shape[2]), preferred_eleme...]
    reshape x1 -> x0, local copies, waits for them, and re-layouts: 5.05 us -> none  [blend_axis(): return blended.reshape(target)]
    unnamed x35 -> x9, local copies, waits for them, and re-layouts: 8.44 us -> 3.47 us
    slice x5 -> x0, local copies, waits for them, and re-layouts: 3.05 us -> none  [the longest x1 1.1 us: context_by_kernel(): padded[:, 15:]]
    ppermute x4 -> x0, waiting for transfers between devices: 2.85 us -> none  [the longest x2 1.59 us: padded_2(): before = lax.ppermute(last, axis, up)]
    another operation x2 -> x0, local copies, waits for them, and re-layouts: 2.82 us -> none  [blend_axis(): jnp.stack([factor * lower_half + (1.0 - factor) * upper_half for factor i...]
  transfers between devices with their start and end apart: 4 -> 0, of which waited for: 2 -> 0; matrix products, arithmetic and copies ran while one was open for 14% -> 0% of each run, Pallas kernels for 71% -> 0%
where the time goes in v2:
time: 156 us; the launch traced here: 155 us
  Pallas kernels  145 us (93%)
  local copies, waits for them, and re-layouts  4.71 us (3%)
  other arithmetic  4.36 us (3%)
    pallas_call x1, Pallas kernels, pyramid(): pl.pallas_call(lambda *refs: pyramid_kernel((rows, lines, window, low_wid...  135 us
    pallas_call x1, Pallas kernels, whole_by_kernels(): pl.pallas_call(lambda *refs: decoder_kernel(strip, *refs), out_shape=jax....  10 us
    unnamed x9, local copies, waits for them, and re-layouts  3.47 us

profile of v2, /device:TPU:1, one launch (start us, length us, event | category | flops | bytes accessed | tf_op | source)
XLA Modules:
  0.0 155.2 jit_solution(1581211026873543307)
XLA Ops:
  0.7 0.1 iota.99
  0.8 0.1 iota.100
  0.8 1.4 select_maximum_fusion
  2.3 0.1 iota.89
  2.4 0.9 copy.15
  3.2 0.8 fusion.7.refs_8_
  4.1 1.0 pad.14.refs_4_
  5.0 1.4 select_convert_fusion.refs_2_
  6.5 0.0 copy-start.1
  6.5 0.0 copy-start.2
  6.5 135.4 %shard_map.140 = (bf16[6,80,256]{2,1,0:T(8,128)(2,1)}, bf16[18,256,256]{2,1,0:T(8,128)(2,1)}) custom-call(bf16[4,128,1024]{2,1,0:T(8,128)(2,1)} %refs_0_.1, bf16[3,9,16,1024]{3,2,1,0:T(8,128)(2,1)} %bitcast.9, bf16[1024,256]{1,0:T(8,128)(2,1)} %refs_2_.1, bf16[1024,256]{1,0:T(8,128)(2,1)} %refs_3_.1, f32[5,256]{1,0:T(8,128)} %refs_4_.1, ...), custom_call_target="tpu_custom_call" | custom-call | flops 7516192768 | bytes 14155776 | tf_op jit(solution)/shard_map/pallas_call | solution.py:465
  141.9 0.0 copy-done.1
  141.9 0.0 copy-done.2
  141.9 0.0 copy-start
  141.9 0.9 copy-done
  142.8 0.0 copy-start.3
  142.8 1.7 %copy-done.3 = bf16[18,256,256]{2,1,0:T(8,128)(2,1)S(1)} copy-done((bf16[18,256,256]{2,1,0:T(8,128)(2,1)S(1)}, bf16[18,256,256]{2,1,0:T(8,128)(2,1)}, u32[]{:S(2)}) %copy-start.3) | copy-done | bytes 2359320
  144.5 10.0 %shard_map.141 = bf16[16,256,256]{2,1,0:T(8,128)(2,1)} custom-call(bf16[6,80,256]{2,1,0:T(8,128)(2,1)S(1)} %copy-done, bf16[18,256,256]{2,1,0:T(8,128)(2,1)S(1)} %copy-done.3, bf16[4,768,160]{2,1,0:T(8,128)(2,1)S(1)} %select_convert_fusion.refs_2_, bf16[3,768,256]{2,1,0:T(8,128)(2,1)S(1)} %bitcast.6, bf16[3,256,256]{2,1,0:T(8,128)(2,1)S(1)} %pad.14.refs_4_, ...), custom_call_target="tpu_custom_call" | custom-call | flops 6442450944 | bytes 4194304 | tf_op jit(solution)/shard_map/pallas_call | solution.py:595
  154.5 0.7 slice_select_fusion
  (9 shorter events, 0.1 us)
Async XLA Ops:
  6.5 135.4 %copy-start.1 = (bf16[9,256,256]{2,1,0:T(8,128)(2,1)S(1)}, bf16[9,256,256]{2,1,0:T(8,128)(2,1)}, u32[]{:S(2)}) copy-start(bf16[9,256,256]{2,1,0:T(8,128)(2,1)} %param.23) | copy-start | bytes 3538948
  6.5 135.4 %copy-start.2 = (f32[256]{0:T(256)S(1)}, f32[256]{0:T(256)}, u32[]{:S(2)}) copy-start(f32[256]{0:T(256)} %param.25) | copy-start | bytes 3076
  141.9 0.9 copy-start
  142.8 1.7 %copy-start.3 = (bf16[18,256,256]{2,1,0:T(8,128)(2,1)S(1)}, bf16[18,256,256]{2,1,0:T(8,128)(2,1)}, u32[]{:S(2)}) copy-start(bf16[18,256,256]{2,1,0:T(8,128)(2,1)} %get-tuple-element.5.refs_1_) | copy-start | bytes 7077892

commit v3 on v2

--- a/solution.py
+++ b/solution.py
@@ -102,11 +102,11 @@
     f_ref, own_ref, one_ref, pool_ref, branch_bias_ref, proj_ref, proj_bias_ref,
     low_ref, low_weight_ref, low_bias_ref,
     out_ref, low_out_ref,
-    wbuf, shifted, sums, row_send, row_recv, merged, chan_recv, total, context, halo,
+    wbuf, maps, shifted, row_send, row_recv, merged, chan_recv, total, context, halo,
     pool_send, pool_recv, pool_line,
-    gather_send, gather_recv, row_ssem, row_rsem, chan_ssem, chan_rsem, halo_ssem, halo_rsem,
+    own_send, gather_send, gather_recv, row_ssem, row_rsem, chan_ssem, chan_rsem, halo_ssem, halo_rsem,
     pool_ssem, pool_rsem,
-    low_edge, low_send, low_recv, low_rows_send, low_rows_recv, low_ssem, low_rsem,
+    maps_ssem, maps_rsem, low_edge, low_send, low_recv, low_rows_send, low_rows_recv, low_ssem, low_rsem,
 ):
     rows, lines, window, low_width = geometry
     fine_rows, fine_cols, low_depth = low_ref.shape
@@ -118,6 +118,14 @@
     chan = lax.axis_index("chan")
     mine_z = me // 4
     mine_y = (me // 2) % 2
+    mine_c = me % 2
+    half = mine_z % 2
+    twin = me + 4 - 8 * half
+    sources = lines // 2
+    own_half = mine_z // sources
+    own_slot = me - own_half * (rows // 2)
+    part = width // 2
+    lanes = pl.ds(pl.multiple_of(half * part, part), part)
     core_peer = me + 1 - 2 * (me % 2)
     y_peer = me + 2 - 4 * mine_y
     chan_peer = 1 - chan
@@ -145,7 +153,12 @@
 
     row_recv[...] = jnp.zeros_like(row_recv)
     low_rows_recv[...] = jnp.zeros_like(low_rows_recv)
-    wbuf[me] = own_ref[...]
+    maps[0] = f_ref[...]
+
+    @pl.when(own_half == half)
+    def _():
+        wbuf[own_slot] = own_ref[...]
+
 
     barrier = pltpu.get_barrier_semaphore()
     for step in range(1, rows):
@@ -155,29 +168,23 @@
     pl.semaphore_signal(barrier, inc=1, device_id={"chan": chan_peer}, device_id_type=MESH)
     pl.semaphore_wait(barrier, rows)
 
-    counter = [0]
-
-    def pass_shard(cond, source, level, target):
-        index = counter[0]
-        counter[0] += 1
-        slot = wbuf.at[source, level]
-        send(
-            cond,
-            remote(slot, slot, gather_send.at[index], gather_recv.at[level, source], {"rows": target}),
-        )
-
-    def shard_here(cond, source, level):
-        arrive(cond, wbuf.at[source, level], gather_recv.at[level, source], gather_send.at[0])
-
-    def both(one, other):
-        return other if one is None else one & other
+    def slot_copy(ref, slot, level, ssem, target):
+        return remote(
+            ref, wbuf.at[slot, level], ssem, gather_recv.at[level, slot], {"rows": target}
+        )
 
     order = list(range(levels))[::-1]
-    for level in order:
-        pass_shard(mine_z + 1 < lines, me, level, me + 4)
-        pass_shard(mine_z > 0, me, level, me - 4)
-        pass_shard(None, me, level, y_peer)
-        pass_shard(None, me, level, core_peer)
+    for turn, level in enumerate(order):
+        for at in range(sources):
+            there = own_half + 2 * at
+            send(
+                there != mine_z,
+                slot_copy(
+                    own_ref.at[level], own_slot, level, own_send.at[level, at], me + 4 * (there - mine_z)
+                ),
+            )
+        if turn == 0:
+            send(None, remote(maps.at[0], maps.at[1], maps_ssem, maps_rsem, {"rows": twin}))
 
     def flat():
         return f_ref[...].reshape(pixels, depth)
@@ -232,15 +239,17 @@
         else:
             total[...] += term
 
-    def shift_level(level):
+    def shift_level(level, which):
         spacing = RATE * (level + 1)
-        pos = lax.broadcasted_iota(jnp.int32, (cols, depth), 0)
-        for row in range(strip):
-            value = f_ref[row].astype(F32)
+
+        @pl.loop(0, strip)
+        def _(row):
+            pos = lax.broadcasted_iota(jnp.int32, (cols, depth), 0)
+            value = maps[which, row].astype(F32)
             before = jnp.where(pos < spacing, 0.0, pltpu.roll(value, spacing, 0))
             after = jnp.where(pos >= cols - spacing, 0.0, pltpu.roll(value, cols - spacing, 0))
-            shifted[level, 0, row] = before.astype(BF16)
-            shifted[level, 1, row] = after.astype(BF16)
+            shifted[level, 0, which, row] = before.astype(BF16)
+            shifted[level, 1, which, row] = after.astype(BF16)
 
     def mapped_low(value):
         return jax.nn.relu(
@@ -263,7 +272,7 @@
     merge(0, jnp.dot(flat(), one_ref[...], preferred_element_type=F32))
     pool_add(0)
     pool_round(1)
-    shift_level(order[0])
+    shift_level(order[0], 0)
     pool_add(1)
     pool_round(2)
 
@@ -296,7 +305,7 @@
             ),
         )
     for level in order[1:]:
-        shift_level(level)
+        shift_level(level, 0)
     pool_add(2)
     pool_line[mine_z] = pool_send[3]
     for step in range(1, lines):
@@ -316,76 +325,119 @@
     project(0, True)
 
     def gather_level(level):
-        for step in range(1, lines):
-            for sign in (-1, 1):
-                source = me + 4 * sign * step
-                here = (mine_z + sign * step >= 0) & (mine_z + sign * step < lines)
-                beyond = here & (mine_z - sign >= 0) & (mine_z - sign < lines)
-                shard_here(here, source, level)
-                pass_shard(beyond, source, level, me - 4 * sign)
-                pass_shard(here, source, level, y_peer)
-                pass_shard(here, source, level, core_peer)
-        for step in range(lines):
-            for sign in (-1, 1) if step else (1,):
-                source = y_peer + 4 * sign * step
-                here = (mine_z + sign * step >= 0) & (mine_z + sign * step < lines)
-                shard_here(here, source, level)
-                pass_shard(here, source, level, core_peer)
-        for line in range(lines):
+        count = [0]
+
+        def forward(slot, target):
+            ssem = gather_send.at[level, count[0]]
+            count[0] += 1
+            send(None, slot_copy(wbuf.at[slot, level], slot, level, ssem, target))
+
+        def here(cond, slot):
+            arrive(cond, wbuf.at[slot, level], gather_recv.at[level, slot], gather_send.at[level, 0])
+
+        near = [
+            jnp.where(mine_z < sources, at, sources - 1 - at) * 4 for at in range(sources)
+        ]
+        for place in near:
+            slot = place + 2 * mine_y + mine_c
+            here((half != own_half) | (slot != own_slot), slot)
+            forward(slot, y_peer)
+            forward(slot, core_peer)
+        for place in near:
+            slot = place + 2 * (1 - mine_y) + mine_c
+            here(None, slot)
+            forward(slot, core_peer)
+        for place in near:
             for y in range(2):
-                shard_here(None, line * 4 + y * 2 + 1 - me % 2, level)
+                here(None, place + 2 * y + 1 - mine_c)
 
     def row_copies(level):
         hop, remain = divmod(RATE * (level + 1), strip)
         found = []
         if remain < strip:
             found.append((0, hop, 0, remain, strip - remain))
-            found.append((1, -hop, remain, 0, strip - remain))
+            found.append((2, -hop, remain, 0, strip - remain))
         if remain > 0:
             found.append((0, hop + 1, strip - remain, 0, remain))
-            found.append((1, -hop - 1, 0, strip - remain, remain))
+            found.append((2, -hop - 1, 0, strip - remain, remain))
         return found
 
-    def compute_level(level):
-        spread = levels * 3
-
-        @pl.loop(0, 3)
-        def _(down):
-            value = None
-            for across in range(3):
-                weight = wbuf[:, level, 3 * down + across].reshape(width, depth)
-                side = f_ref[...] if across == 1 else shifted[level, across // 2]
-                term = dot_t(side.reshape(pixels, depth), weight)
-                value = term if value is None else value + term
-            sums[level, down] = value
-
-        for at, down in enumerate((0, 2)):
-            row_send[level, at] = sums[level, down].astype(BF16).reshape(strip, cols, width)
-        for index, (at, offset, first, into, count) in enumerate(row_copies(level)):
-            cond = (me + offset >= 0) & (me + offset < rows)
+    def compute_strip(level, which):
+        def weight(tap):
+            return wbuf[:, level, tap].reshape(part, depth)
+
+        outer, centre = None, None
+        for across in range(3):
+            side = maps[which] if across == 1 else shifted[level, across // 2, which]
+            side = side.reshape(pixels, depth)
+            pair = jnp.concatenate([weight(across), weight(6 + across)], axis=0)
+            term = dot_t(side, pair)
+            outer = term if outer is None else outer + term
+            term = dot_t(side, weight(3 + across))
+            centre = term if centre is None else centre + term
+        row_send[level, which, 0] = outer[:, :part].astype(BF16).reshape(strip, cols, part)
+        row_send[level, which, 2] = outer[:, part:].astype(BF16).reshape(strip, cols, part)
+        centre = centre.astype(BF16).reshape(strip, cols, part)
+        if which == 0:
+            row_recv[level, 1, :, :, lanes] = centre
+        else:
+            row_send[level, which, 1] = centre
+
+    def send_strip(level, which):
+        base = me if which == 0 else twin
+        for index, (down, offset, first, into, count) in enumerate(row_copies(level)):
+            there = base + offset
+            inside = (there >= 0) & (there < rows)
+            source = row_send.at[level, which, down, pl.ds(first, count)]
+            target = row_recv.at[level, down, pl.ds(into, count), :, lanes]
+            rsem = row_rsem.at[level, index, half]
+            away = remote(source, target, row_ssem.at[level, index, which], rsem, {"rows": there})
+            if which == 1 and abs(offset) == 4:
+                home = pltpu.make_async_copy(source, target, rsem)
+                pl.when(there == me)(home.start)
+                send(inside & (there != me), away)
+            else:
+                send(inside, away)
+        if which == 1:
             send(
-                cond,
+                None,
                 remote(
-                    row_send.at[level, at, pl.ds(first, count)],
-                    row_recv.at[level, at, pl.ds(into, count)],
-                    row_ssem.at[level, index],
-                    row_rsem.at[level, index],
-                    {"rows": me + offset},
+                    row_send.at[level, 1, 1],
+                    row_recv.at[level, 1, :, :, lanes],
+                    row_ssem.at[level, 4, 1],
+                    row_rsem.at[level, 4, half],
+                    {"rows": twin},
                 ),
             )
 
+    def compute_level(level):
+        for which in (1, 0):
+            compute_strip(level, which)
+            send_strip(level, which)
+
     def finish_level(level):
-        for index, (at, offset, first, into, count) in enumerate(row_copies(level)):
+        for index, (down, offset, first, into, count) in enumerate(row_copies(level)):
             cond = (me - offset >= 0) & (me - offset < rows)
-            arrive(
-                cond, row_recv.at[level, at, pl.ds(into, count)], row_rsem.at[level, index], row_ssem.at[level, index]
-            )
-        value = sums[level, 1].reshape(strip, cols, width)
-        value = value + row_recv[level, 0].astype(F32) + row_recv[level, 1].astype(F32)
-        merge(level + 1, value)
+            for side in range(2):
+                arrive(
+                    cond,
+                    row_recv.at[level, down, pl.ds(into, count), :, pl.ds(side * part, part)],
+                    row_rsem.at[level, index, side],
+                    row_ssem.at[level, index, 0],
+                )
+        others = pl.ds(pl.multiple_of((1 - half) * part, part), part)
+        arrive(
+            None, row_recv.at[level, 1, :, :, others], row_rsem.at[level, 4, 1 - half], row_ssem.at[level, 4, 0]
+        )
+        value = row_recv[level, 0].astype(F32) + row_recv[level, 1].astype(F32)
+        merge(level + 1, value + row_recv[level, 2].astype(F32))
 
     for turn, level in enumerate(order):
         gather_level(level)
+        if turn == 0:
+            arrive(None, maps.at[1], maps_rsem, maps_ssem)
+            for each in order:
+                shift_level(each, 1)
         compute_level(level)
         if turn >= 1:
             finish_level(order[turn - 1])
@@ -453,7 +505,7 @@
     window = cols // 2 + 16
     pixels = strip * cols
     own = jnp.swapaxes(w_rate, 2, 3)
-    sends = levels * (4 + 2 * 3 * (lines - 1) + 2 * lines)
+    sources = lines // 2
     fine_rows, fine_cols, low_depth = low_features.shape
     low_width = w_low.shape[1]
     packed = pl.cdiv(3 * low_width, 128) * 128
@@ -471,11 +523,11 @@
         in_specs=[vmem] * 10,
         out_specs=(vmem, vmem),
         scratch_shapes=[
-            pltpu.VMEM((rows, levels, taps, shard, depth), BF16),
-            pltpu.VMEM((levels, 2, strip, cols, depth), BF16),
-            pltpu.VMEM((levels, 3, pixels, width), F32),
-            pltpu.VMEM((levels, 2, strip, cols, width), BF16),
-            pltpu.VMEM((levels, 2, strip, cols, width), BF16),
+            pltpu.VMEM((rows // 2, levels, taps, shard, depth), BF16),
+            pltpu.VMEM((2, strip, cols, depth), BF16),
+            pltpu.VMEM((levels, 2, 2, strip, cols, depth), BF16),
+            pltpu.VMEM((levels, 2, 3, strip, cols, width // 2), BF16),
+            pltpu.VMEM((levels, 3, strip, cols, width), BF16),
             pltpu.VMEM((levels + 1, strip, cols, width), BF16),
             pltpu.VMEM((levels + 1, strip, window, width), BF16),
             pltpu.VMEM((strip * window, width), F32),
@@ -484,16 +536,19 @@
             pltpu.VMEM((4, 8, width), F32),
             pltpu.VMEM((3, 8, width), F32),
             pltpu.VMEM((lines, 8, width), F32),
-            dma((sends,)),
-            dma((levels, rows)),
-            dma((levels, 4)),
-            dma((levels, 4)),
+            dma((levels, sources)),
+            dma((levels, 3 * sources)),
+            dma((levels, rows // 2)),
+            dma((levels, 5, 2)),
+            dma((levels, 5, 2)),
             dma((levels + 1,)),
             dma((levels + 1,)),
             dma((2,)),
             dma((2,)),
             dma((3 + 2 * lines,)),
             dma((3 + lines,)),
+            dma,
+            dma,
             pltpu.VMEM((fine_rows, low_depth), F32),
             pltpu.VMEM((fine_rows, packed), F32),
             pltpu.VMEM((fine_rows, packed), F32),
@@ -682,7 +737,8 @@
     chan_count = lax.axis_size("chan")
     fits = (
         chan_count == 2
-        and rows_count % 4 == 0
+        and rows_count % 8 == 0
+        and w_one.shape[1] % 256 == 0
         and w_rate.shape[3] % 16 == 0
         and features.shape[1] % 32 == 0
         and features.shape[2] % 128 == 0

time: 156 us -> 129 us (0.83)
  Pallas kernels: 145 us -> 117 us
    pallas_call x1, Pallas kernels: 135 us -> 107 us  [pyramid(): pl.pallas_call(lambda *refs: pyramid_kernel((rows, lines, window, low_wid...]
where the time goes in v3:
time: 129 us; the launch traced here: 127 us
  Pallas kernels  117 us (91%)
  local copies, waits for them, and re-layouts  4.71 us (4%)
  other arithmetic  4.36 us (3%)
    pallas_call x1, Pallas kernels, pyramid(): pl.pallas_call(lambda *refs: pyramid_kernel((rows, lines, window, low_wid...  107 us
    pallas_call x1, Pallas kernels, whole_by_kernels(): pl.pallas_call(lambda *refs: decoder_kernel(strip, *refs), out_shape=jax....  10 us
    unnamed x9, local copies, waits for them, and re-layouts  3.47 us

profile of v3, /device:TPU:1, one launch (start us, length us, event | category | flops | bytes accessed | tf_op | source)
XLA Modules:
  0.0 126.7 jit_solution(1786784147105379965)
XLA Ops:
  0.7 0.1 iota.99
  0.8 0.1 iota.100
  0.8 1.4 %select_maximum_fusion = f32[256]{0:T(256)} fusion(f32[48]{0:T(128)} %param.22), kind=kLoop, calls=%fused_computation.29 | loop fusion | flops 1536 | bytes 1216 | tf_op jit(solution)/shard_map/concatenate | solution.py:514
  2.3 0.1 iota.89
  2.4 0.9 copy.15
  3.2 0.8 fusion.7.refs_8_
  4.1 1.0 pad.14.refs_4_
  5.0 1.4 %select_convert_fusion.refs_2_ = bf16[4,768,160]{2,1,0:T(8,128)(2,1)S(1)} fusion(f32[4]{0:T(128)S(1)} %get-tuple-element.13, f32[4]{0:T(128)S(1)} %get-tuple-element.12, s32[768]{0:T(1024)S(1)} %get-tuple-element.11, s32[768]{0:T(1024)S(1)} %get-tuple-element.10, s32[]{:T(128)S(6)} %mul.28, s32[768]{0:T(1024)S(1)} %add.87, s32[768]{0:T(1024)S(1)} %get-tuple-element.9, ...), kind=kLoop, calls=%fused_computation.7 | loop fusion | flops 15237120 | bytes 999240 | tf_op jit(solution)/shard_map/convert_element_type | solution.py:626
  6.5 0.0 copy-start.1
  6.5 0.0 copy-start.2
  6.5 106.9 %shard_map.140 = (bf16[6,80,256]{2,1,0:T(8,128)(2,1)}, bf16[18,256,256]{2,1,0:T(8,128)(2,1)}) custom-call(bf16[4,128,1024]{2,1,0:T(8,128)(2,1)} %refs_0_.1, bf16[3,9,16,1024]{3,2,1,0:T(8,128)(2,1)} %bitcast.9, bf16[1024,256]{1,0:T(8,128)(2,1)} %refs_2_.1, bf16[1024,256]{1,0:T(8,128)(2,1)} %refs_3_.1, f32[5,256]{1,0:T(8,128)} %refs_4_.1, ...), custom_call_target="tpu_custom_call" | custom-call | flops 7516192768 | bytes 14155776 | tf_op jit(solution)/shard_map/pallas_call | solution.py:517
  113.4 0.0 copy-done.1
  113.4 0.0 copy-done.2
  113.4 0.0 copy-start
  113.4 0.9 copy-done
  114.4 0.0 copy-start.3
  114.4 1.7 %copy-done.3 = bf16[18,256,256]{2,1,0:T(8,128)(2,1)S(1)} copy-done((bf16[18,256,256]{2,1,0:T(8,128)(2,1)S(1)}, bf16[18,256,256]{2,1,0:T(8,128)(2,1)}, u32[]{:S(2)}) %copy-start.3) | copy-done | bytes 2359320
  116.0 10.0 %shard_map.141 = bf16[16,256,256]{2,1,0:T(8,128)(2,1)} custom-call(bf16[6,80,256]{2,1,0:T(8,128)(2,1)S(1)} %copy-done, bf16[18,256,256]{2,1,0:T(8,128)(2,1)S(1)} %copy-done.3, bf16[4,768,160]{2,1,0:T(8,128)(2,1)S(1)} %select_convert_fusion.refs_2_, bf16[3,768,256]{2,1,0:T(8,128)(2,1)S(1)} %bitcast.6, bf16[3,256,256]{2,1,0:T(8,128)(2,1)S(1)} %pad.14.refs_4_, ...), custom_call_target="tpu_custom_call" | custom-call | flops 6442450944 | bytes 4194304 | tf_op jit(solution)/shard_map/pallas_call | solution.py:650
  126.0 0.7 slice_select_fusion
  (9 shorter events, 0.1 us)
Async XLA Ops:
  6.5 106.9 %copy-start.1 = (bf16[9,256,256]{2,1,0:T(8,128)(2,1)S(1)}, bf16[9,256,256]{2,1,0:T(8,128)(2,1)}, u32[]{:S(2)}) copy-start(bf16[9,256,256]{2,1,0:T(8,128)(2,1)} %param.23) | copy-start | bytes 3538948
  6.5 106.9 %copy-start.2 = (f32[256]{0:T(256)S(1)}, f32[256]{0:T(256)}, u32[]{:S(2)}) copy-start(f32[256]{0:T(256)} %param.25) | copy-start | bytes 3076
  113.4 0.9 copy-start
  114.4 1.7 %copy-start.3 = (bf16[18,256,256]{2,1,0:T(8,128)(2,1)S(1)}, bf16[18,256,256]{2,1,0:T(8,128)(2,1)}, u32[]{:S(2)}) copy-start(bf16[18,256,256]{2,1,0:T(8,128)(2,1)} %get-tuple-element.5.refs_1_) | copy-start | bytes 7077892

commit v4 on v3

--- a/solution.py
+++ b/solution.py
@@ -1,5 +1,6 @@
 import jax
 import jax.numpy as jnp
+import numpy as np
 from jax import lax
 from jax.experimental import pallas as pl
 from jax.experimental.pallas import tpu as pltpu
@@ -174,7 +175,7 @@
         )
 
     order = list(range(levels))[::-1]
-    for turn, level in enumerate(order):
+    for level in order:
         for at in range(sources):
             there = own_half + 2 * at
             send(
@@ -183,21 +184,23 @@
                     own_ref.at[level], own_slot, level, own_send.at[level, at], me + 4 * (there - mine_z)
                 ),
             )
-        if turn == 0:
-            send(None, remote(maps.at[0], maps.at[1], maps_ssem, maps_rsem, {"rows": twin}))
+    send(None, remote(maps.at[0], maps.at[1], maps_ssem, maps_rsem, {"rows": twin}))
 
     def flat():
         return f_ref[...].reshape(pixels, depth)
 
-    local = jnp.zeros((8, depth), F32)
-    for row in range(strip):
-        block = f_ref[row].astype(F32).reshape(cols // 8, 8, depth)
-        local = local + jnp.sum(block, axis=0)
-    local = jnp.broadcast_to(jnp.sum(local, axis=0, keepdims=True), (8, depth))
-    pool_send[0] = jnp.dot(
-        local, pool_ref[...].astype(F32), precision=lax.Precision.HIGHEST, preferred_element_type=F32
-    )
     peers = ({"chan": chan_peer}, {"rows": core_peer}, {"rows": y_peer})
+
+    def pool_start():
+        local = jnp.zeros((8, depth), F32)
+        for row in range(strip):
+            block = f_ref[row].astype(F32).reshape(cols // 8, 8, depth)
+            local = local + jnp.sum(block, axis=0)
+        local = jnp.broadcast_to(jnp.sum(local, axis=0, keepdims=True), (8, depth))
+        pool_send[0] = jnp.dot(
+            local, pool_ref[...].astype(F32), precision=lax.Precision.HIGHEST, preferred_element_type=F32
+        )
+        pool_round(0)
 
     def pool_round(turn):
         send(
@@ -256,100 +259,94 @@
             jnp.dot(value, low_weight_ref[...], preferred_element_type=F32) + low_bias_ref[...]
         )
 
-    @pl.loop(0, fine_rows)
-    def _(row):
-        first = low_ref[row, 0:16, :].astype(F32)
-        last = low_ref[row, fine_cols - 16 : fine_cols, :].astype(F32)
-        low_edge[pl.ds(row, 1), :] = jnp.where(chan == 0, last[15:16], first[0:1])
-
-    low_send[...] = mapped_low(low_edge[...].astype(BF16))
-    send(
-        None,
-        remote(low_send, low_recv, low_ssem.at[0], low_rsem.at[0], {"chan": chan_peer}),
-    )
-
-    pool_round(0)
-    merge(0, jnp.dot(flat(), one_ref[...], preferred_element_type=F32))
-    pool_add(0)
-    pool_round(1)
-    shift_level(order[0], 0)
-    pool_add(1)
-    pool_round(2)
-
-    arrive(None, low_recv, low_rsem.at[0], low_ssem.at[0])
-
-    @pl.loop(0, fine_rows)
-    def _(row):
-        value = mapped_low(low_ref[row])
-        pos = lax.broadcasted_iota(jnp.int32, (fine_cols, packed), 0)
-        lane = lax.broadcasted_iota(jnp.int32, (fine_cols, packed), 1)
-        outer = low_recv[pl.ds(row, 1), :]
-        left = jnp.where(chan == 0, 0.0, outer)
-        right = jnp.where(chan == 0, outer, 0.0)
-        before = jnp.where(pos == 0, left, pltpu.roll(value, 1, 0))
-        after = jnp.where(pos == fine_cols - 1, right, pltpu.roll(value, fine_cols - 1, 0))
-        value = jnp.where(lane < low_width, before, jnp.where(lane < 2 * low_width, value, after))
-        low_out_ref[row + 1] = value.astype(BF16)
-
-    low_rows_send[0] = low_out_ref[1]
-    low_rows_send[1] = low_out_ref[fine_rows]
-    for at, offset in enumerate((-1, 1)):
+    def low_edges():
+        @pl.loop(0, fine_rows)
+        def _(row):
+            first = low_ref[row, 0:16, :].astype(F32)
+            last = low_ref[row, fine_cols - 16 : fine_cols, :].astype(F32)
+            low_edge[pl.ds(row, 1), :] = jnp.where(chan == 0, last[15:16], first[0:1])
+
+        low_send[...] = mapped_low(low_edge[...].astype(BF16))
         send(
-            (me + offset >= 0) & (me + offset < rows),
-            remote(
-                low_rows_send.at[at],
-                low_rows_recv.at[at],
-                low_ssem.at[1 + at],
-                low_rsem.at[1 + at],
-                {"rows": me + offset},
-            ),
-        )
-    for level in order[1:]:
-        shift_level(level, 0)
-    pool_add(2)
-    pool_line[mine_z] = pool_send[3]
-    for step in range(1, lines):
-        for at, sign in enumerate((1, -1)):
-            there = mine_z + sign * step
-            cond = (there >= 0) & (there < lines)
+            None,
+            remote(low_send, low_recv, low_ssem.at[0], low_rsem.at[0], {"chan": chan_peer}),
+        )
+
+    def low_maps():
+        arrive(None, low_recv, low_rsem.at[0], low_ssem.at[0])
+
+        @pl.loop(0, fine_rows)
+        def _(row):
+            value = mapped_low(low_ref[row])
+            pos = lax.broadcasted_iota(jnp.int32, (fine_cols, packed), 0)
+            lane = lax.broadcasted_iota(jnp.int32, (fine_cols, packed), 1)
+            outer = low_recv[pl.ds(row, 1), :]
+            left = jnp.where(chan == 0, 0.0, outer)
+            right = jnp.where(chan == 0, outer, 0.0)
+            before = jnp.where(pos == 0, left, pltpu.roll(value, 1, 0))
+            after = jnp.where(pos == fine_cols - 1, right, pltpu.roll(value, fine_cols - 1, 0))
+            value = jnp.where(lane < low_width, before, jnp.where(lane < 2 * low_width, value, after))
+            low_out_ref[row + 1] = value.astype(BF16)
+
+        low_rows_send[0] = low_out_ref[1]
+        low_rows_send[1] = low_out_ref[fine_rows]
+        for at, offset in enumerate((-1, 1)):
             send(
-                cond,
+                (me + offset >= 0) & (me + offset < rows),
                 remote(
-                    pool_send.at[3],
-                    pool_line.at[mine_z],
-                    pool_ssem.at[3 + 2 * (step - 1) + at],
-                    pool_rsem.at[3 + mine_z],
-                    {"rows": me + 4 * sign * step},
+                    low_rows_send.at[at],
+                    low_rows_recv.at[at],
+                    low_ssem.at[1 + at],
+                    low_rsem.at[1 + at],
+                    {"rows": me + offset},
                 ),
             )
-    project(0, True)
-
-    def gather_level(level):
-        count = [0]
-
-        def forward(slot, target):
-            ssem = gather_send.at[level, count[0]]
-            count[0] += 1
-            send(None, slot_copy(wbuf.at[slot, level], slot, level, ssem, target))
-
-        def here(cond, slot):
-            arrive(cond, wbuf.at[slot, level], gather_recv.at[level, slot], gather_send.at[level, 0])
-
-        near = [
-            jnp.where(mine_z < sources, at, sources - 1 - at) * 4 for at in range(sources)
-        ]
-        for place in near:
+
+    def pool_lines():
+        pool_line[mine_z] = pool_send[3]
+        for step in range(1, lines):
+            for at, sign in enumerate((1, -1)):
+                there = mine_z + sign * step
+                cond = (there >= 0) & (there < lines)
+                send(
+                    cond,
+                    remote(
+                        pool_send.at[3],
+                        pool_line.at[mine_z],
+                        pool_ssem.at[3 + 2 * (step - 1) + at],
+                        pool_rsem.at[3 + mine_z],
+                        {"rows": me + 4 * sign * step},
+                    ),
+                )
+
+    near = [jnp.where(mine_z < sources, at, sources - 1 - at) * 4 for at in range(sources)]
+
+    def forward(slot, level, index, target):
+        send(
+            None,
+            slot_copy(wbuf.at[slot, level], slot, level, gather_send.at[level, index], target),
+        )
+
+    def here(cond, slot, level):
+        arrive(cond, wbuf.at[slot, level], gather_recv.at[level, slot], gather_send.at[level, 0])
+
+    def own_column(level):
+        for at, place in enumerate(near):
             slot = place + 2 * mine_y + mine_c
-            here((half != own_half) | (slot != own_slot), slot)
-            forward(slot, y_peer)
-            forward(slot, core_peer)
-        for place in near:
+            here((half != own_half) | (slot != own_slot), slot, level)
+            forward(slot, level, 2 * at, y_peer)
+            forward(slot, level, 2 * at + 1, core_peer)
+
+    def other_column(level):
+        for at, place in enumerate(near):
             slot = place + 2 * (1 - mine_y) + mine_c
-            here(None, slot)
-            forward(slot, core_peer)
+            here(None, slot, level)
+            forward(slot, level, 2 * sources + at, core_peer)
+
+    def other_core(level):
         for place in near:
             for y in range(2):
-                here(None, place + 2 * y + 1 - mine_c)
+                here(None, place + 2 * y + 1 - mine_c, level)
 
     def row_copies(level):
         hop, remain = divmod(RATE * (level + 1), strip)
@@ -410,10 +407,9 @@
                 ),
             )
 
-    def compute_level(level):
-        for which in (1, 0):
-            compute_strip(level, which)
-            send_strip(level, which)
+    def work(level, which):
+        compute_strip(level, which)
+        send_strip(level, which)
 
     def finish_level(level):
         for index, (down, offset, first, into, count) in enumerate(row_copies(level)):
@@ -432,17 +428,44 @@
         value = row_recv[level, 0].astype(F32) + row_recv[level, 1].astype(F32)
         merge(level + 1, value + row_recv[level, 2].astype(F32))
 
-    for turn, level in enumerate(order):
-        gather_level(level)
-        if turn == 0:
-            arrive(None, maps.at[1], maps_rsem, maps_ssem)
-            for each in order:
-                shift_level(each, 1)
-        compute_level(level)
-        if turn >= 1:
-            finish_level(order[turn - 1])
-        if turn >= 2:
-            project(order[turn - 2] + 1, False)
+    assert levels == 3
+    one, two, three = order
+    low_edges()
+    pool_start()
+    shift_level(one, 0)
+    own_column(one)
+    merge(0, jnp.dot(flat(), one_ref[...], preferred_element_type=F32))
+    pool_add(0)
+    pool_round(1)
+    shift_level(two, 0)
+    own_column(two)
+    other_column(one)
+    pool_add(1)
+    pool_round(2)
+    shift_level(three, 0)
+    low_maps()
+    own_column(three)
+    other_core(one)
+    other_column(two)
+    work(one, 0)
+    pool_add(2)
+    pool_lines()
+    other_core(two)
+    other_column(three)
+    work(two, 0)
+    project(0, True)
+    arrive(None, maps.at[1], maps_rsem, maps_ssem)
+    shift_level(one, 1)
+    work(one, 1)
+    shift_level(two, 1)
+    work(two, 1)
+    finish_level(one)
+    shift_level(three, 1)
+    other_core(three)
+    work(three, 1)
+    work(three, 0)
+    finish_level(two)
+    project(one + 1, False)
 
     for at, (offset, place) in enumerate(((-1, fine_rows + 1), (1, 0))):
         cond = (me - offset >= 0) & (me - offset < rows)
@@ -462,9 +485,9 @@
     constant = jnp.dot(pooled, proj_ref[4 * width :, :], preferred_element_type=F32)
     constant = constant[0:1, :] + proj_bias_ref[...]
 
-    finish_level(order[-1])
-    for level in order[-2:]:
-        project(level + 1, False)
+    project(two + 1, False)
+    finish_level(three)
+    project(three + 1, False)
 
     value = jax.nn.relu(total[...] + constant).astype(BF16).reshape(strip, window, width)
     context[...] = value
@@ -609,21 +632,23 @@
     out_ref[...] = total.astype(BF16).reshape(block, fine_cols, width)
 
 
-def blend_matrices(half, window, chan_index):
+def blend_table(half, window, chan_count):
     fine_cols = 4 * half
-    shape = (4, 3, fine_cols, 2, window)
-    phase, across, pos, lower, col = (lax.broadcasted_iota(jnp.int32, shape, d) for d in range(5))
+    shape = (chan_count, 4, 3, fine_cols, 2, window)
+    chan, phase, across, pos, lower, col = np.indices(shape, sparse=True)
     place = pos + across - 1
     pair, col_phase = (place + 2) // 4, (place + 2) % 4
-    first = jnp.clip(chan_index * half + pair - 1, 0, 2 * half - 1) - chan_index * (2 * half - window)
-    second = jnp.clip(chan_index * half + pair, 0, 2 * half - 1) - chan_index * (2 * half - window)
-    col_upper = 0.875 - 0.25 * col_phase.astype(F32)
-    factor = jnp.where(col == first, col_upper, 0.0) + jnp.where(col == second, 1.0 - col_upper, 0.0)
-    row_upper = 0.875 - 0.25 * phase.astype(F32)
-    factor = factor * jnp.where(lower == 0, row_upper, 1.0 - row_upper)
-    whole = chan_index * fine_cols + place
-    factor = jnp.where((whole >= 0) & (whole < 2 * fine_cols), factor, 0.0)
-    return factor.astype(BF16).reshape(4, 3 * fine_cols, 2 * window)
+    origin = chan * (chan_count * half - window)
+    last = chan_count * half - 1
+    first = np.clip(chan * half + pair - 1, 0, last) - origin
+    second = np.clip(chan * half + pair, 0, last) - origin
+    col_upper = 0.875 - 0.25 * col_phase
+    factor = np.where(col == first, col_upper, 0.0) + np.where(col == second, 1.0 - col_upper, 0.0)
+    row_upper = 0.875 - 0.25 * phase
+    factor = factor * np.where(lower == 0, row_upper, 1.0 - row_upper)
+    whole = chan * fine_cols + place
+    factor = np.where((whole >= 0) & (whole < chan_count * fine_cols), factor, 0.0)
+    return factor.astype(np.float32).astype(BF16).reshape(chan_count, 4, 3 * fine_cols, 2 * window)
 
 
 def whole_by_kernels(
@@ -643,7 +668,8 @@
     up_weight = w_dec_up.reshape(3, 3 * depth, width)
     low_weight = w_dec_low.reshape(3, -1, width)
     low_weight = jnp.pad(low_weight, ((0, 0), (0, packed - low_weight.shape[1]), (0, 0)))
-    blend = blend_matrices(half, window, chan_index)
+    table = blend_table(half, window, 2)
+    blend = jnp.where(chan_index == 0, table[0], table[1])
     whole = pl.BlockSpec(memory_space=pltpu.VMEM)
     block = 4
     pixels = fine_rows * fine_cols

time: 129 us -> 136 us (1.054)
  Pallas kernels: 117 us -> 124 us
    pallas_call x1, Pallas kernels: 107 us -> 114 us  [pyramid(): pl.pallas_call(lambda *refs: pyramid_kernel((rows, lines, window, low_wid...]
    select_n x0 -> x1, other arithmetic: none -> 1.58 us  [whole_by_kernels(): blend = jnp.where(chan_index == 0, table[0], table[1])]
    convert_element_type x1 -> x0, other arithmetic: 1.43 us -> none  [blend_matrices(): return factor.astype(BF16).reshape(4, 3 * fine_cols, 2 * window)]
where the time goes in v4:
time: 136 us; the launch traced here: 134 us
  Pallas kernels  124 us (91%)
  other arithmetic  4.46 us (3%)
  local copies, waits for them, and re-layouts  4.43 us (3%)
    pallas_call x1, Pallas kernels, pyramid(): pl.pallas_call(lambda *refs: pyramid_kernel((rows, lines, window, low_wid...  114 us
    pallas_call x1, Pallas kernels, whole_by_kernels(): pl.pallas_call(lambda *refs: decoder_kernel(strip, *refs), out_shape=jax....  10 us
    unnamed x9, local copies, waits for them, and re-layouts  3.47 us

profile of v4, /device:TPU:1, one launch (start us, length us, event | category | flops | bytes accessed | tf_op | source)
XLA Modules:
  0.0 133.6 jit_solution(12553871006407295619)
XLA Ops:
  0.6 1.4 %select_maximum_fusion = f32[256]{0:T(256)} fusion(f32[48]{0:T(128)} %param.24), kind=kLoop, calls=%fused_computation.8 | loop fusion | flops 1536 | bytes 1216 | tf_op jit(solution)/shard_map/concatenate | solution.py:537
  2.0 0.9 copy.17
  2.9 0.8 fusion.4.refs_8_
  3.7 1.0 pad.14.refs_4_
  4.7 1.6 %broadcast_select_fusion.refs_2_ = bf16[4,768,160]{2,1,0:T(8,128)(2,1)S(1)} fusion(bf16[4,768,160]{2,1,0:T(8,128)(2,1)} %constant.14.clone, bf16[4,768,160]{2,1,0:T(8,128)(2,1)} %constant.15.clone, pred[]{:T(512)S(6)} %eq.4), kind=kLoop, calls=%fused_computation | loop fusion | flops 491520 | bytes 2949121 | tf_op jit(solution)/shard_map/jit(_where)/select_n | solution.py:672
  6.3 0.0 copy-start.1
  6.3 0.0 copy-start.2
  6.3 114.1 %shard_map.158 = (bf16[6,80,256]{2,1,0:T(8,128)(2,1)}, bf16[18,256,256]{2,1,0:T(8,128)(2,1)}) custom-call(bf16[4,128,1024]{2,1,0:T(8,128)(2,1)} %refs_0_.1, bf16[3,9,16,1024]{3,2,1,0:T(8,128)(2,1)} %bitcast.9, bf16[1024,256]{1,0:T(8,128)(2,1)} %refs_2_.1, bf16[1024,256]{1,0:T(8,128)(2,1)} %refs_3_.1, f32[5,256]{1,0:T(8,128)} %refs_4_.1, ...), custom_call_target="tpu_custom_call" | custom-call | flops 7516192768 | bytes 14155776 | tf_op jit(solution)/shard_map/pallas_call | solution.py:540
  120.3 0.0 copy-done.1
  120.3 0.0 copy-done.2
  120.4 0.0 copy-start
  120.4 0.9 copy-done
  121.3 0.0 copy-start.3
  121.3 1.7 %copy-done.3 = bf16[18,256,256]{2,1,0:T(8,128)(2,1)S(1)} copy-done((bf16[18,256,256]{2,1,0:T(8,128)(2,1)S(1)}, bf16[18,256,256]{2,1,0:T(8,128)(2,1)}, u32[]{:S(2)}) %copy-start.3) | copy-done | bytes 2359320
  123.0 10.0 %shard_map.159 = bf16[16,256,256]{2,1,0:T(8,128)(2,1)} custom-call(bf16[6,80,256]{2,1,0:T(8,128)(2,1)S(1)} %copy-done, bf16[18,256,256]{2,1,0:T(8,128)(2,1)S(1)} %copy-done.3, bf16[4,768,160]{2,1,0:T(8,128)(2,1)S(1)} %broadcast_select_fusion.refs_2_, bf16[3,768,256]{2,1,0:T(8,128)(2,1)S(1)} %bitcast.6, bf16[3,256,256]{2,1,0:T(8,128)(2,1)S(1)} %pad.14.refs_4_, ...), custom_call_target="tpu_custom_call" | custom-call | flops 6442450944 | bytes 4194304 | tf_op jit(solution)/shard_map/pallas_call | solution.py:676
  133.0 0.7 slice_select_fusion
Async XLA Ops:
  6.3 114.1 %copy-start.1 = (bf16[9,256,256]{2,1,0:T(8,128)(2,1)S(1)}, bf16[9,256,256]{2,1,0:T(8,128)(2,1)}, u32[]{:S(2)}) copy-start(bf16[9,256,256]{2,1,0:T(8,128)(2,1)} %param.25) | copy-start | bytes 3538948
  6.3 114.1 %copy-start.2 = (f32[256]{0:T(256)S(1)}, f32[256]{0:T(256)}, u32[]{:S(2)}) copy-start(f32[256]{0:T(256)} %param.27) | copy-start | bytes 3076
  120.4 0.9 copy-start
  121.3 1.7 %copy-start.3 = (bf16[18,256,256]{2,1,0:T(8,128)(2,1)S(1)}, bf16[18,256,256]{2,1,0:T(8,128)(2,1)}, u32[]{:S(2)}) copy-start(bf16[18,256,256]{2,1,0:T(8,128)(2,1)} %get-tuple-element.5.refs_1_) | copy-start | bytes 7077892

commit v5 on v4

--- a/solution.py
+++ b/solution.py
@@ -1,6 +1,5 @@
 import jax
 import jax.numpy as jnp
-import numpy as np
 from jax import lax
 from jax.experimental import pallas as pl
 from jax.experimental.pallas import tpu as pltpu
@@ -175,7 +174,7 @@
         )
 
     order = list(range(levels))[::-1]
-    for level in order:
+    for turn, level in enumerate(order):
         for at in range(sources):
             there = own_half + 2 * at
             send(
@@ -184,7 +183,8 @@
                     own_ref.at[level], own_slot, level, own_send.at[level, at], me + 4 * (there - mine_z)
                 ),
             )
-    send(None, remote(maps.at[0], maps.at[1], maps_ssem, maps_rsem, {"rows": twin}))
+        if turn == 0:
+            send(None, remote(maps.at[0], maps.at[1], maps_ssem, maps_rsem, {"rows": twin}))
 
     def flat():
         return f_ref[...].reshape(pixels, depth)
@@ -438,29 +438,29 @@
     pool_add(0)
     pool_round(1)
     shift_level(two, 0)
-    own_column(two)
     other_column(one)
     pool_add(1)
     pool_round(2)
     shift_level(three, 0)
     low_maps()
-    own_column(three)
     other_core(one)
-    other_column(two)
     work(one, 0)
     pool_add(2)
     pool_lines()
-    other_core(two)
-    other_column(three)
-    work(two, 0)
-    project(0, True)
     arrive(None, maps.at[1], maps_rsem, maps_ssem)
     shift_level(one, 1)
+    own_column(two)
     work(one, 1)
     shift_level(two, 1)
+    other_column(two)
+    project(0, True)
+    shift_level(three, 1)
+    other_core(two)
     work(two, 1)
+    own_column(three)
+    work(two, 0)
+    other_column(three)
     finish_level(one)
-    shift_level(three, 1)
     other_core(three)
     work(three, 1)
     work(three, 0)
@@ -632,23 +632,21 @@
     out_ref[...] = total.astype(BF16).reshape(block, fine_cols, width)
 
 
-def blend_table(half, window, chan_count):
+def blend_matrices(half, window, chan_index):
     fine_cols = 4 * half
-    shape = (chan_count, 4, 3, fine_cols, 2, window)
-    chan, phase, across, pos, lower, col = np.indices(shape, sparse=True)
+    shape = (4, 3, fine_cols, 2, window)
+    phase, across, pos, lower, col = (lax.broadcasted_iota(jnp.int32, shape, d) for d in range(5))
     place = pos + across - 1
     pair, col_phase = (place + 2) // 4, (place + 2) % 4
-    origin = chan * (chan_count * half - window)
-    last = chan_count * half - 1
-    first = np.clip(chan * half + pair - 1, 0, last) - origin
-    second = np.clip(chan * half + pair, 0, last) - origin
-    col_upper = 0.875 - 0.25 * col_phase
-    factor = np.where(col == first, col_upper, 0.0) + np.where(col == second, 1.0 - col_upper, 0.0)
-    row_upper = 0.875 - 0.25 * phase
-    factor = factor * np.where(lower == 0, row_upper, 1.0 - row_upper)
-    whole = chan * fine_cols + place
-    factor = np.where((whole >= 0) & (whole < chan_count * fine_cols), factor, 0.0)
-    return factor.astype(np.float32).astype(BF16).reshape(chan_count, 4, 3 * fine_cols, 2 * window)
+    first = jnp.clip(chan_index * half + pair - 1, 0, 2 * half - 1) - chan_index * (2 * half - window)
+    second = jnp.clip(chan_index * half + pair, 0, 2 * half - 1) - chan_index * (2 * half - window)
+    col_upper = 0.875 - 0.25 * col_phase.astype(F32)
+    factor = jnp.where(col == first, col_upper, 0.0) + jnp.where(col == second, 1.0 - col_upper, 0.0)
+    row_upper = 0.875 - 0.25 * phase.astype(F32)
+    factor = factor * jnp.where(lower == 0, row_upper, 1.0 - row_upper)
+    whole = chan_index * fine_cols + place
+    factor = jnp.where((whole >= 0) & (whole < 2 * fine_cols), factor, 0.0)
+    return factor.astype(BF16).reshape(4, 3 * fine_cols, 2 * window)
 
 
 def whole_by_kernels(
@@ -668,8 +666,7 @@
     up_weight = w_dec_up.reshape(3, 3 * depth, width)
     low_weight = w_dec_low.reshape(3, -1, width)
     low_weight = jnp.pad(low_weight, ((0, 0), (0, packed - low_weight.shape[1]), (0, 0)))
-    table = blend_table(half, window, 2)
-    blend = jnp.where(chan_index == 0, table[0], table[1])
+    blend = blend_matrices(half, window, chan_index)
     whole = pl.BlockSpec(memory_space=pltpu.VMEM)
     block = 4
     pixels = fine_rows * fine_cols

time: 136 us -> 130 us (0.956); the launches traced: 134 us -> 129 us
  Pallas kernels: 124 us -> 119 us
    pallas_call x1, Pallas kernels: 114 us -> 109 us  [pyramid(): pl.pallas_call(lambda *refs: pyramid_kernel((rows, lines, window, low_wid...]
    select_n x1 -> x0, other arithmetic: 1.58 us -> none  [whole_by_kernels(): blend = jnp.where(chan_index == 0, table[0], table[1])]
    convert_element_type x0 -> x1, other arithmetic: none -> 1.43 us  [blend_matrices(): return factor.astype(BF16).reshape(4, 3 * fine_cols, 2 * window)]
where the time goes in v5:
time: 130 us; the launch traced here: 129 us
  Pallas kernels  119 us (92%)
  local copies, waits for them, and re-layouts  4.71 us (4%)
  other arithmetic  4.36 us (3%)
    pallas_call x1, Pallas kernels, pyramid(): pl.pallas_call(lambda *refs: pyramid_kernel((rows, lines, window, low_wid...  109 us
    pallas_call x1, Pallas kernels, whole_by_kernels(): pl.pallas_call(lambda *refs: decoder_kernel(strip, *refs), out_shape=jax....  10 us
    unnamed x9, local copies, waits for them, and re-layouts  3.47 us

profile of v5, /device:TPU:1, one launch (start us, length us, event | category | flops | bytes accessed | tf_op | source)
XLA Modules:
  0.0 129.2 jit_solution(6674879065048383037)
XLA Ops:
  0.7 0.1 iota.99
  0.8 0.1 iota.100
  0.8 1.4 %select_maximum_fusion = f32[256]{0:T(256)} fusion(f32[48]{0:T(128)} %param.22), kind=kLoop, calls=%fused_computation.29 | loop fusion | flops 1536 | bytes 1216 | tf_op jit(solution)/shard_map/concatenate | solution.py:537
  2.3 0.1 iota.89
  2.4 0.9 copy.15
  3.2 0.8 fusion.7.refs_8_
  4.1 1.0 pad.14.refs_4_
  5.0 1.4 %select_convert_fusion.refs_2_ = bf16[4,768,160]{2,1,0:T(8,128)(2,1)S(1)} fusion(f32[4]{0:T(128)S(1)} %get-tuple-element.13, f32[4]{0:T(128)S(1)} %get-tuple-element.12, s32[768]{0:T(1024)S(1)} %get-tuple-element.11, s32[768]{0:T(1024)S(1)} %get-tuple-element.10, s32[]{:T(128)S(6)} %mul.28, s32[768]{0:T(1024)S(1)} %add.87, s32[768]{0:T(1024)S(1)} %get-tuple-element.9, ...), kind=kLoop, calls=%fused_computation.7 | loop fusion | flops 15237120 | bytes 999240 | tf_op jit(solution)/shard_map/convert_element_type | solution.py:649
  6.5 0.0 copy-start.1
  6.5 0.0 copy-start.2
  6.5 109.5 %shard_map.140 = (bf16[6,80,256]{2,1,0:T(8,128)(2,1)}, bf16[18,256,256]{2,1,0:T(8,128)(2,1)}) custom-call(bf16[4,128,1024]{2,1,0:T(8,128)(2,1)} %refs_0_.1, bf16[3,9,16,1024]{3,2,1,0:T(8,128)(2,1)} %bitcast.9, bf16[1024,256]{1,0:T(8,128)(2,1)} %refs_2_.1, bf16[1024,256]{1,0:T(8,128)(2,1)} %refs_3_.1, f32[5,256]{1,0:T(8,128)} %refs_4_.1, ...), custom_call_target="tpu_custom_call" | custom-call | flops 7516192768 | bytes 14155776 | tf_op jit(solution)/shard_map/pallas_call | solution.py:540
  115.9 0.0 copy-done.1
  116.0 0.0 copy-done.2
  116.0 0.0 copy-start
  116.0 0.9 copy-done
  116.9 0.0 copy-start.3
  116.9 1.7 %copy-done.3 = bf16[18,256,256]{2,1,0:T(8,128)(2,1)S(1)} copy-done((bf16[18,256,256]{2,1,0:T(8,128)(2,1)S(1)}, bf16[18,256,256]{2,1,0:T(8,128)(2,1)}, u32[]{:S(2)}) %copy-start.3) | copy-done | bytes 2359320
  118.6 10.0 %shard_map.141 = bf16[16,256,256]{2,1,0:T(8,128)(2,1)} custom-call(bf16[6,80,256]{2,1,0:T(8,128)(2,1)S(1)} %copy-done, bf16[18,256,256]{2,1,0:T(8,128)(2,1)S(1)} %copy-done.3, bf16[4,768,160]{2,1,0:T(8,128)(2,1)S(1)} %select_convert_fusion.refs_2_, bf16[3,768,256]{2,1,0:T(8,128)(2,1)S(1)} %bitcast.6, bf16[3,256,256]{2,1,0:T(8,128)(2,1)S(1)} %pad.14.refs_4_, ...), custom_call_target="tpu_custom_call" | custom-call | flops 6442450944 | bytes 4194304 | tf_op jit(solution)/shard_map/pallas_call | solution.py:673
  128.6 0.7 slice_select_fusion
  (9 shorter events, 0.1 us)
Async XLA Ops:
  6.5 109.5 %copy-start.1 = (bf16[9,256,256]{2,1,0:T(8,128)(2,1)S(1)}, bf16[9,256,256]{2,1,0:T(8,128)(2,1)}, u32[]{:S(2)}) copy-start(bf16[9,256,256]{2,1,0:T(8,128)(2,1)} %param.23) | copy-start | bytes 3538948
  6.5 109.5 %copy-start.2 = (f32[256]{0:T(256)S(1)}, f32[256]{0:T(256)}, u32[]{:S(2)}) copy-start(f32[256]{0:T(256)} %param.25) | copy-start | bytes 3076
  116.0 0.9 copy-start
  116.9 1.7 %copy-start.3 = (bf16[18,256,256]{2,1,0:T(8,128)(2,1)S(1)}, bf16[18,256,256]{2,1,0:T(8,128)(2,1)}, u32[]{:S(2)}) copy-start(bf16[18,256,256]{2,1,0:T(8,128)(2,1)} %get-tuple-element.5.refs_1_) | copy-start | bytes 7077892
